TPU v7x, 512 devices: a whole 4x4x16 slice. The times are simulated.
512 devices in a mesh: af: 32 (over x, z_hi, core), gx: 4 (over z_lo), gy: 4 (over y).
Axes of the slice: x: 4, y: 4, z: 16 (z_hi: 4, z_lo: 4; z = z_hi * 4 + z_lo), core: 2. Of those that a mesh axis runs over, the one named last changes fastest.
Arguments:
- background: float32 [32, 2, 2, 3, 16, 32, 128], P('af', None, None, None, 'gx', 'gy'), may hold values from -6 to 6
- conductivity: float32 [3, 16, 32, 128], P(None, 'gx', 'gy'), may hold values from 0.1 to 1
- perturbation: float32 [3, 16, 32, 128], P(None, 'gx', 'gy'), may hold values from -15 to 15
- coupling: float32 [32], P('af'), may hold values from 0.3 to 3
- relaxation: float32 [2, 3], replicated, may hold values from 0.4 to 1.4
- receivers: int32 [1024], replicated, may hold values from 0 to 65535, as said below
- weights: float32 [32, 1024], P('af'), may hold values from 0.5 to 2
Outputs:
- hess_vec: float32 [3, 16, 32, 128], P(None, 'gx', 'gy', 'af')
Inputs may be any that keep to these rules, and one draw needn't show every extreme that they name: `receivers`: distinct flat cell indices (x 32 + y) * 128 + z of the whole grid.
All inputs are finite; a program needn't handle non-finite values.
Results may differ from a plain program's by a relative error of at most 0.0003.
Values sent between devices are 32-bit elements; how exact they have to be, the bound alone decides.
A program may use at most 64 MiB of HBM per device.

v0:
```python
import jax
import jax.numpy as jnp
from jax import lax
from jax.sharding import PartitionSpec as P


def extended_2(block, sides, width):
    for axis, dim in sides:
        count = lax.axis_size(axis)
        forward = [(i, i + 1) for i in range(count - 1)]
        backward = [(target, source) for source, target in forward]
        low = lax.ppermute(
            lax.slice_in_dim(block, block.shape[dim] - width, None, axis=dim), axis, forward
        )
        high = lax.ppermute(lax.slice_in_dim(block, 0, width, axis=dim), axis, backward)
        block = jnp.concatenate([low, block, high], axis=dim)
    return block


def curl_curl(padded):
    width_x = padded.shape[-3] - 2
    width_y = padded.shape[-2] - 2
    edge_x = padded[..., 0, :, :, :]
    edge_y = padded[..., 1, :, :, :]
    edge_z = padded[..., 2, :, :, :]

    def along_x(values):
        return (
            values[..., 1 : width_x + 2, : width_y + 1, :]
            - values[..., : width_x + 1, : width_y + 1, :]
        )

    def along_y(values):
        return (
            values[..., : width_x + 1, 1 : width_y + 2, :]
            - values[..., : width_x + 1, : width_y + 1, :]
        )

    def along_z(values):
        middle = values[..., : width_x + 1, : width_y + 1, :]
        raised = jnp.concatenate([middle[..., 1:], jnp.zeros_like(middle[..., :1])], axis=-1)
        return raised - middle

    face_x = along_y(edge_z) - along_z(edge_y)
    face_y = along_z(edge_x) - along_x(edge_z)
    face_z = along_x(edge_y) - along_y(edge_x)

    def back_x(values):
        return values[..., :width_x, 1:, :] - values[..., 1:, 1:, :]

    def back_y(values):
        return values[..., 1:, :width_y, :] - values[..., 1:, 1:, :]

    def back_z(values):
        middle = values[..., 1:, 1:, :]
        lowered = jnp.concatenate([jnp.zeros_like(middle[..., :1]), middle[..., :-1]], axis=-1)
        return lowered - middle

    curl_x = back_z(face_y) - back_y(face_z)
    curl_y = back_x(face_z) - back_z(face_x)
    curl_z = back_y(face_x) - back_x(face_y)
    return jnp.stack([curl_x, curl_y, curl_z], axis=-4)


def apply_operator(padded, fields, conductivity, coupled):
    curled = curl_curl(padded)
    damping = coupled * conductivity
    real_part = curled[..., 0, :, :, :, :] - damping * fields[..., 1, :, :, :, :]
    imag_part = curled[..., 1, :, :, :, :] + damping * fields[..., 0, :, :, :, :]
    return jnp.stack([real_part, imag_part], axis=-5)


def operate(fields, conductivity, coupled):
    padded = extended_2(fields, (("gx", 4), ("gy", 5)), 1)
    return apply_operator(padded, fields, conductivity, coupled)


def inner_sums(mapped, residual):
    mapped_real = mapped[..., 0, :, :, :, :]
    mapped_imag = mapped[..., 1, :, :, :, :]
    resid_real = residual[..., 0, :, :, :, :]
    resid_imag = residual[..., 1, :, :, :, :]
    axes_all = (-4, -3, -2, -1)
    dot_real = jnp.sum(mapped_real * resid_real + mapped_imag * resid_imag, axis=axes_all)
    dot_imag = jnp.sum(mapped_real * resid_imag - mapped_imag * resid_real, axis=axes_all)
    squares = jnp.sum(mapped_real * mapped_real + mapped_imag * mapped_imag, axis=axes_all)
    return lax.psum((dot_real, dot_imag, squares), ("gx", "gy"))


def complex_times(alpha_real, alpha_imag, fields):
    field_real = fields[..., 0, :, :, :, :]
    field_imag = fields[..., 1, :, :, :, :]
    real_part = alpha_real * field_real - alpha_imag * field_imag
    imag_part = alpha_real * field_imag + alpha_imag * field_real
    return jnp.stack([real_part, imag_part], axis=-5)


def relaxed_solve(source, coeffs, conductivity, coupled):
    answer = jnp.zeros_like(source)
    residual = source
    for turn_index in range(coeffs.shape[0]):
        mapped = operate(residual, conductivity, coupled)
        dot_real, dot_imag, squares = inner_sums(mapped, residual)
        factor = coeffs[turn_index] / (squares + 1e-06)
        alpha_real = (factor * dot_real)[..., None, None, None, None]
        alpha_imag = (factor * dot_imag)[..., None, None, None, None]
        answer = answer + complex_times(alpha_real, alpha_imag, residual)
        residual = residual - complex_times(alpha_real, alpha_imag, mapped)
    return answer


def station_cells(receivers, weights, width_x, width_y, layers):
    span_y = width_y * lax.axis_size("gy")
    plane_size = span_y * layers
    pos_x = receivers // plane_size - lax.axis_index("gx") * width_x
    pos_y = receivers // layers % span_y - lax.axis_index("gy") * width_y
    pos_z = receivers % layers
    inside = (pos_x >= 0) & (pos_x < width_x) & (pos_y >= 0) & (pos_y < width_y)
    cell_count = width_x * width_y * layers
    local_index = jnp.where(inside, (pos_x * width_y + pos_y) * layers + pos_z, cell_count)
    station_weight = (
        jnp.zeros((weights.shape[0], cell_count), jnp.float32)
        .at[:, local_index]
        .add(weights, mode="drop")
    )
    return station_weight.reshape(weights.shape[0], width_x, width_y, layers)


def polarization_term(field_bg, conductivity, perturbation, coupled, relaxation, station_mask):
    weighted = coupled * perturbation
    source = jnp.stack(
        [weighted * field_bg[..., 1, :, :, :, :], -(weighted * field_bg[..., 0, :, :, :, :])],
        axis=-5,
    )
    incremental = relaxed_solve(source, relaxation[0], conductivity, coupled)
    adjoint = relaxed_solve(incremental * station_mask, relaxation[1], conductivity, coupled)
    products = coupled * (
        field_bg[..., 0, :, :, :, :] * adjoint[..., 1, :, :, :, :]
        + field_bg[..., 1, :, :, :, :] * adjoint[..., 0, :, :, :, :]
    )
    return jnp.sum(products, axis=(0, 1))


def per_device(background, conductivity, perturbation, coupling, relaxation, receivers, weights):
    width_x = background.shape[4]
    width_y = background.shape[5]
    layers = background.shape[6]
    coupled = coupling.reshape(-1, 1, 1, 1, 1, 1)
    station_weight = station_cells(receivers, weights, width_x, width_y, layers)
    selector = jnp.array([1.0, 1.0, 0.0], jnp.float32)
    station_mask = (station_weight[:, None] * selector[None, :, None, None, None])[:, None, None]
    gradient_term = polarization_term(
        background, conductivity, perturbation, coupled, relaxation, station_mask
    )
    return lax.psum_scatter(gradient_term, "af", scatter_dimension=3, tiled=True)


def solution(mesh):
    placed = (
        P("af", None, None, None, "gx", "gy", None),
        P(None, "gx", "gy", None),
        P(None, "gx", "gy", None),
        P("af"),
        P(),
        P(),
        P("af", None),
    )
    return jax.shard_map(
        per_device, mesh=mesh, in_specs=placed, out_specs=P(None, "gx", "gy", "af"), check_vma=False
    )
```

profile of v0, /device:TPU:1, one launch (start us, length us, event | category | flops | bytes accessed | tf_op | source)
XLA Modules:
  0.0 528.1 jit_solution(4721874157151396263)
XLA Ops:
  2.9 5.0 collective-permute-start
  10.4 4.0 collective-permute-start.2
  16.3 38.4 %all-reduce.30 = (f32[1,2]{1,0:T(1,128)S(1)}, f32[1,2]{1,0:T(1,128)S(1)}, f32[1,2]{1,0:T(1,128)S(1)}) all-reduce(f32[1,2]{1,0:T(1,128)S(1)} %bitcast.360, f32[1,2]{1,0:T(1,128)S(1)} %bitcast.359, f32[1,2]{1,0:T(1,128)S(1)} %bitcast.358), channel_id=1, replica_groups=mesh['af'=32,'gx'=4,'gy'=4] {'gx','gy'}, use_global_device_ids=true, to_apply=%region_1.2 | all-reduce | flops 6 | bytes 48 | tf_op jit(solution)/shard_map/psum | solution.py:87
  58.2 3.5 collective-permute-done.5
  61.8 1.3 collective-permute-start.7
  63.1 4.0 collective-permute-start.6
  69.0 32.8 %all-reduce.29 = (f32[1,2]{1,0:T(1,128)S(1)}, f32[1,2]{1,0:T(1,128)S(1)}, f32[1,2]{1,0:T(1,128)S(1)}) all-reduce(f32[1,2]{1,0:T(1,128)S(1)} %bitcast.363, f32[1,2]{1,0:T(1,128)S(1)} %bitcast.362, f32[1,2]{1,0:T(1,128)S(1)} %bitcast.361), channel_id=1, replica_groups=mesh['af'=32,'gx'=4,'gy'=4] {'gx','gy'}, use_global_device_ids=true, to_apply=%region_7.8 | all-reduce | flops 6 | bytes 48 | tf_op jit(solution)/shard_map/psum | solution.py:87
  102.6 1.3 collective-permute-start.8
  103.9 6.1 %scatter_custom_fusion = f32[4096]{0:T(1024)S(1)} fusion(s32[1024]{0:T(1024)S(1)} %compare_select_fusion, f32[1024]{0:T(1024)} %bitcast.376, f32[]{:T(128)} %constant.59.clone.1), kind=kCustom, calls=%fused_computation.288 | custom fusion | flops 1024 | bytes 16896 | tf_op jit(solution)/shard_map/scatter-add | solution.py:124
  111.4 3.5 collective-permute-done.9
  116.2 4.0 collective-permute-start.10
  122.1 32.6 %all-reduce.28 = (f32[1,2]{1,0:T(1,128)S(1)}, f32[1,2]{1,0:T(1,128)S(1)}, f32[1,2]{1,0:T(1,128)S(1)}) all-reduce(f32[1,2]{1,0:T(1,128)S(1)} %bitcast.366, f32[1,2]{1,0:T(1,128)S(1)} %bitcast.365, f32[1,2]{1,0:T(1,128)S(1)} %bitcast.364), channel_id=1, replica_groups=mesh['af'=32,'gx'=4,'gy'=4] {'gx','gy'}, use_global_device_ids=true, to_apply=%region_13.14 | all-reduce | flops 6 | bytes 48 | tf_op jit(solution)/shard_map/psum | solution.py:87
  158.3 3.7 collective-permute-done.13
  163.4 4.0 collective-permute-start.14
  169.2 32.6 %all-reduce.27 = (f32[1,2]{1,0:T(1,128)S(1)}, f32[1,2]{1,0:T(1,128)S(1)}, f32[1,2]{1,0:T(1,128)S(1)}) all-reduce(f32[1,2]{1,0:T(1,128)S(1)} %bitcast.369, f32[1,2]{1,0:T(1,128)S(1)} %bitcast.368, f32[1,2]{1,0:T(1,128)S(1)} %bitcast.367), channel_id=1, replica_groups=mesh['af'=32,'gx'=4,'gy'=4] {'gx','gy'}, use_global_device_ids=true, to_apply=%region_20.21 | all-reduce | flops 6 | bytes 48 | tf_op jit(solution)/shard_map/psum | solution.py:87
  204.0 1.3 collective-permute-start.17
  205.4 3.7 collective-permute-done.17
  210.5 4.0 collective-permute-start.18
  216.3 32.6 %all-reduce.26 = (f32[1,2]{1,0:T(1,128)S(1)}, f32[1,2]{1,0:T(1,128)S(1)}, f32[1,2]{1,0:T(1,128)S(1)}) all-reduce(f32[1,2]{1,0:T(1,128)S(1)} %bitcast.372, f32[1,2]{1,0:T(1,128)S(1)} %bitcast.371, f32[1,2]{1,0:T(1,128)S(1)} %bitcast.370), channel_id=1, replica_groups=mesh['af'=32,'gx'=4,'gy'=4] {'gx','gy'}, use_global_device_ids=true, to_apply=%region_26.27 | all-reduce | flops 6 | bytes 48 | tf_op jit(solution)/shard_map/psum | solution.py:87
  251.1 4.0 collective-permute-start.20
  257.6 4.0 collective-permute-start.22
  261.6 1.3 dynamic-slice
  264.5 31.9 %all-reduce.25 = (f32[1,2]{1,0:T(1,128)S(1)}, f32[1,2]{1,0:T(1,128)S(1)}, f32[1,2]{1,0:T(1,128)S(1)}) all-reduce(f32[1,2]{1,0:T(1,128)S(1)} %bitcast.373, f32[1,2]{1,0:T(1,128)S(1)} %bitcast.375, f32[1,2]{1,0:T(1,128)S(1)} %bitcast.374), channel_id=1, replica_groups=mesh['af'=32,'gx'=4,'gy'=4] {'gx','gy'}, use_global_device_ids=true, to_apply=%region_32.33 | all-reduce | flops 6 | bytes 48 | tf_op jit(solution)/shard_map/psum | solution.py:87
  297.5 230.0 %all-reduce.24 = f32[3,4,8,128]{2,3,1,0:T(8,128)S(1)} all-reduce(f32[3,4,8,128]{2,3,1,0:T(8,128)S(1)} %copy.127), channel_id=2, replica_groups=mesh['af'=32,'gx'=4,'gy'=4] {'af'}, use_global_device_ids=true, to_apply=%region_38.39.clone | all-reduce | flops 12288 | bytes 98304
  (172 shorter events, 36.2 us)
Async XLA Ops:
  1.6 6.3 %collective-permute-start.1 = (f32[1,2,2,3,1,8,128]{6,5,4,3,1,2,0:T(8,128)S(1)}, f32[1,2,2,3,1,8,128]{6,5,4,3,1,2,0:T(8,128)S(1)}, u32[]{:S(2)}, u32[]{:S(2)}) collective-permute-start(f32[1,2,2,3,1,8,128]{6,5,4,3,1,2,0:T(8,128)S(1)} %get-tuple-element.145), channel_id=1, source_target_pairs={{4,0},{8,4},{12,8},{5,1},{9,5},{13,9},{6,2},{10,6},{14,10},{7,3},{... | collective-permute-start | bytes 147464 | tf_op jit(solution)/shard_map/ppermute | solution.py:15
  2.9 6.2 %collective-permute-start = (f32[1,2,2,3,1,8,128]{6,5,4,3,1,2,0:T(8,128)S(1)}, f32[1,2,2,3,1,8,128]{6,5,4,3,1,2,0:T(8,128)S(1)}, u32[]{:S(2)}, u32[]{:S(2)}) collective-permute-start(f32[1,2,2,3,1,8,128]{6,5,4,3,1,2,0:T(8,128)S(1)} %get-tuple-element.144), channel_id=1, source_target_pairs={{0,4},{4,8},{8,12},{1,5},{5,9},{9,13},{2,6},{6,10},{10,14},{3,7},{... | collective-permute-start | bytes 147464 | tf_op jit(solution)/shard_map/ppermute | solution.py:12
  9.1 6.0 %collective-permute-start.3 = (f32[1,2,2,3,6,1,128]{6,5,4,3,1,2,0:T(1,128)S(1)}, f32[1,2,2,3,6,1,128]{6,5,4,3,1,2,0:T(1,128)S(1)}, u32[]{:S(2)}, u32[]{:S(2)}) collective-permute-start(f32[1,2,2,3,6,1,128]{6,5,4,3,1,2,0:T(1,128)S(1)} %get-tuple-element.98), channel_id=1, source_target_pairs={{1,0},{2,1},{3,2},{5,4},{6,5},{7,6},{9,8},{10,9},{11,10},{13,12},{... | collective-permute-start | bytes 110600 | tf_op jit(solution)/shard_map/ppermute | solution.py:15
  10.4 5.0 collective-permute-start.2
  55.6 2.6 collective-permute-start.4
  56.9 4.8 collective-permute-start.5
  61.8 5.3 %collective-permute-start.7 = (f32[1,2,2,3,6,1,128]{6,5,4,1,2,3,0:T(1,128)S(1)}, f32[1,2,2,3,6,1,128]{6,5,4,1,2,3,0:T(1,128)S(1)}, u32[]{:S(2)}, u32[]{:S(2)}) collective-permute-start(f32[1,2,2,3,6,1,128]{6,5,4,1,2,3,0:T(1,128)S(1)} %get-tuple-element.96), channel_id=1, source_target_pairs={{1,0},{2,1},{3,2},{5,4},{6,5},{7,6},{9,8},{10,9},{11,10},{13,12},{... | collective-permute-start | bytes 110600 | tf_op jit(solution)/shard_map/ppermute | solution.py:15
  63.1 5.0 collective-permute-start.6
  102.6 8.7 %collective-permute-start.8 = (f32[1,2,2,3,1,8,128]{6,5,4,1,2,3,0:T(8,128)S(1)}, f32[1,2,2,3,1,8,128]{6,5,4,1,2,3,0:T(8,128)S(1)}, u32[]{:S(2)}, u32[]{:S(2)}) collective-permute-start(f32[1,2,2,3,1,8,128]{6,5,4,1,2,3,0:T(8,128)S(1)} %copy.179), channel_id=1, source_target_pairs={{0,4},{4,8},{8,12},{1,5},{5,9},{9,13},{2,6},{6,10},{10,14},{3,7},{... | collective-permute-start | bytes 147464 | tf_op jit(solution)/shard_map/ppermute | solution.py:12
  110.0 4.8 collective-permute-start.9
  114.9 5.4 %collective-permute-start.11 = (f32[1,2,2,3,6,1,128]{6,5,4,1,2,3,0:T(1,128)S(1)}, f32[1,2,2,3,6,1,128]{6,5,4,1,2,3,0:T(1,128)S(1)}, u32[]{:S(2)}, u32[]{:S(2)}) collective-permute-start(f32[1,2,2,3,6,1,128]{6,5,4,1,2,3,0:T(1,128)S(1)} %get-tuple-element.94), channel_id=1, source_target_pairs={{1,0},{2,1},{3,2},{5,4},{6,5},{7,6},{9,8},{10,9},{11,10},{13,12},{... | collective-permute-start | bytes 110600 | tf_op jit(solution)/shard_map/ppermute | solution.py:15
  116.2 5.0 collective-permute-start.10
  155.6 2.6 collective-permute-start.12
  156.9 5.1 collective-permute-start.13
  162.1 5.3 %collective-permute-start.15 = (f32[1,2,2,3,6,1,128]{6,5,4,1,2,3,0:T(1,128)S(1)}, f32[1,2,2,3,6,1,128]{6,5,4,1,2,3,0:T(1,128)S(1)}, u32[]{:S(2)}, u32[]{:S(2)}) collective-permute-start(f32[1,2,2,3,6,1,128]{6,5,4,1,2,3,0:T(1,128)S(1)} %get-tuple-element.92), channel_id=1, source_target_pairs={{1,0},{2,1},{3,2},{5,4},{6,5},{7,6},{9,8},{10,9},{11,10},{13,12},{... | collective-permute-start | bytes 110600 | tf_op jit(solution)/shard_map/ppermute | solution.py:15
  163.4 5.0 collective-permute-start.14
  202.7 2.6 collective-permute-start.16
  204.0 5.1 collective-permute-start.17
  209.2 5.3 %collective-permute-start.19 = (f32[1,2,2,3,6,1,128]{6,5,4,1,2,3,0:T(1,128)S(1)}, f32[1,2,2,3,6,1,128]{6,5,4,1,2,3,0:T(1,128)S(1)}, u32[]{:S(2)}, u32[]{:S(2)}) collective-permute-start(f32[1,2,2,3,6,1,128]{6,5,4,1,2,3,0:T(1,128)S(1)} %get-tuple-element.90), channel_id=1, source_target_pairs={{1,0},{2,1},{3,2},{5,4},{6,5},{7,6},{9,8},{10,9},{11,10},{13,12},{... | collective-permute-start | bytes 110600 | tf_op jit(solution)/shard_map/ppermute | solution.py:15
  210.5 5.0 collective-permute-start.18
  249.8 5.3 %collective-permute-start.21 = (f32[1,2,2,3,1,8,128]{6,5,4,3,1,2,0:T(8,128)S(1)}, f32[1,2,2,3,1,8,128]{6,5,4,3,1,2,0:T(8,128)S(1)}, u32[]{:S(2)}, u32[]{:S(2)}) collective-permute-start(f32[1,2,2,3,1,8,128]{6,5,4,3,1,2,0:T(8,128)S(1)} %get-tuple-element.117), channel_id=1, source_target_pairs={{4,0},{8,4},{12,8},{5,1},{9,5},{13,9},{6,2},{10,6},{14,10},{7,3},{... | collective-permute-start | bytes 147464 | tf_op jit(solution)/shard_map/ppermute | solution.py:15
  251.1 5.2 collective-permute-start.20
  256.3 7.2 %collective-permute-start.23 = (f32[1,2,2,3,6,1,128]{6,5,4,3,1,2,0:T(1,128)S(1)}, f32[1,2,2,3,6,1,128]{6,5,4,3,1,2,0:T(1,128)S(1)}, u32[]{:S(2)}, u32[]{:S(2)}) collective-permute-start(f32[1,2,2,3,6,1,128]{6,5,4,3,1,2,0:T(1,128)S(1)} %get-tuple-element.88), channel_id=1, source_target_pairs={{1,0},{2,1},{3,2},{5,4},{6,5},{7,6},{9,8},{10,9},{11,10},{13,12},{... | collective-permute-start | bytes 110600 | tf_op jit(solution)/shard_map/ppermute | solution.py:15
  257.6 5.9 %collective-permute-start.22 = (f32[1,2,2,3,6,1,128]{6,5,4,3,1,2,0:T(1,128)S(1)}, f32[1,2,2,3,6,1,128]{6,5,4,3,1,2,0:T(1,128)S(1)}, u32[]{:S(2)}, u32[]{:S(2)}) collective-permute-start(f32[1,2,2,3,6,1,128]{6,5,4,3,1,2,0:T(1,128)S(1)} %get-tuple-element.87), channel_id=1, source_target_pairs={{0,1},{1,2},{2,3},{4,5},{5,6},{6,7},{8,9},{9,10},{10,11},{12,13},{... | collective-permute-start | bytes 110600 | tf_op jit(solution)/shard_map/ppermute | solution.py:12
  (4 other events, 12.2 us)
where the time goes:
time: 536 us; the launch traced here: 528 us
  blocking collectives  431 us (80%)
  starting transfers between devices  53.6 us (10%)
  waiting for transfers between devices  21.2 us (4%)
  other arithmetic  15.3 us (3%)
    unnamed x1, blocking collectives  230 us
    psum x6, blocking collectives, inner_sums(): return lax.psum((dot_real, dot_imag, squares), ('gx', 'gy'))  201 us
    ppermute x12, starting transfers between devices, extended_2(): lax.ppermute(lax.slice_in_dim(block, block.shape[dim] - width, None, axis...  38.1 us
    ppermute x12, starting transfers between devices, extended_2(): lax.ppermute(lax.slice_in_dim(block, 0, width, axis=dim), axis, backward)  15.5 us
    ppermute x12, waiting for transfers between devices, extended_2(): lax.ppermute(lax.slice_in_dim(block, 0, width, axis=dim), axis, backward)  14.4 us
  transfers between devices with their start and end apart: 24, of which 11 were waited for; matrix products, arithmetic and copies ran while one was open for 2% of the time, Pallas kernels for 0%

commit v1 on v0

v1 whole, which is shorter than its diff:
```python
import functools

import jax
import jax.numpy as jnp
from jax import lax
from jax.experimental import pallas as pl
from jax.experimental.pallas import tpu as pltpu
from jax.sharding import PartitionSpec as P

MESH = pl.DeviceIdType.MESH
HALO = 3
X0 = 3
Y0 = 4
ROWS = 16


def halo_table(wx, wy):
    return (
        (1, 0, 0, 3, -3, 0, 0, wy),
        (-1, 0, 0, 3, wx, wx + 3, 0, wy),
        (0, 1, 0, 3, 0, wx, -3, 0),
        (0, -1, 0, 3, 0, wx, wy, wy + 3),
        (1, 1, 0, 3, -2, 0, -2, 0),
        (-1, -1, 0, 3, wx, wx + 2, wy, wy + 2),
        (1, -1, 0, 3, -3, 0, wy, wy + 3),
        (-1, 1, 0, 3, wx, wx + 3, -3, 0),
    )


def damping_table(wx, wy):
    return (
        (1, 0, 0, 3, -2, 0, 0, wy),
        (-1, 0, 0, 3, wx, wx + 2, 0, wy),
        (0, 1, 0, 3, 0, wx, -2, 0),
        (0, -1, 0, 3, 0, wx, wy, wy + 2),
        (1, 1, 0, 3, -2, 0, -2, 0),
        (-1, -1, 0, 3, wx, wx + 2, wy, wy + 2),
        (1, -1, 0, 3, -2, 0, wy, wy + 2),
        (-1, 1, 0, 3, wx, wx + 2, -2, 0),
    )


def frame1_table(wx, wy):
    return (
        (1, 0, 0, 2, -3, -2, 0, wy),
        (-1, 0, 1, 2, wx + 2, wx + 3, 0, wy),
        (0, 1, 0, 2, 0, wx, -3, -2),
        (0, -1, 0, 1, 0, wx, wy + 2, wy + 3),
        (1, -1, 0, 1, -3, 0, wy, wy + 3),
        (-1, 1, 1, 2, wx, wx + 3, -3, 0),
    )


def frame2_table(wx, wy):
    return (
        (1, 0, 0, 2, -3, -1, 0, wy),
        (-1, 0, 0, 2, wx + 1, wx + 3, 0, wy),
        (0, 1, 0, 2, 0, wx, -3, -1),
        (0, -1, 0, 2, 0, wx, wy + 1, wy + 3),
        (1, 1, 0, 2, -2, 0, -2, 0),
        (-1, -1, 0, 2, wx, wx + 2, wy, wy + 2),
        (1, -1, 0, 2, -3, 0, wy, wy + 3),
        (-1, 1, 0, 2, wx, wx + 3, -3, 0),
    )


def cmul(a, b):
    return a[0] * b[0] - a[1] * b[1], a[0] * b[1] + a[1] * b[0]


def cadd(a, b):
    return a[0] + b[0], a[1] + b[1]


def csub(a, b):
    return a[0] - b[0], a[1] - b[1]


def conj(a):
    return a[0], -a[1]


def solve_coefficients(gram, factors):
    one = (jnp.ones_like(gram[0, 0][0]), jnp.zeros_like(gram[0, 0][0]))
    zero = (jnp.zeros_like(one[0]), jnp.zeros_like(one[0]))
    rho = [one]
    total = [zero, zero, zero]
    for k in range(3):
        mapped = []
        for j in range(k + 2):
            if j == 0:
                mapped.append(rho[0])
            elif j <= k:
                mapped.append(cadd(rho[j - 1], rho[j]))
            else:
                mapped.append(rho[j - 1])
        dot = zero
        square = zero[0]
        for j in range(k + 2):
            inner = None
            for l in range(k + 1):
                term = cmul(rho[l], gram[j, l])
                inner = term if inner is None else cadd(inner, term)
            dot = cadd(dot, cmul(conj(mapped[j]), inner))
            inner = None
            for l in range(k + 2):
                term = cmul(mapped[l], gram[j, l])
                inner = term if inner is None else cadd(inner, term)
            square = square + (mapped[j][0] * inner[0] + mapped[j][1] * inner[1])
        factor = factors[k] / (jnp.maximum(square, 0.0) + 1e-6)
        alpha = (factor * dot[0], factor * dot[1])
        for j in range(k + 1):
            total[j] = cadd(total[j], cmul(alpha, rho[j]))
        rho = [
            csub(rho[j], cmul(alpha, mapped[j]))
            if j <= k
            else csub(zero, cmul(alpha, mapped[j]))
            for j in range(k + 2)
        ]
    return total


def kernel(
    sizes,
    bg,
    cond,
    pert,
    coup,
    relax,
    rec,
    wts,
    out,
    bgv,
    condv,
    pertv,
    v0,
    v1,
    v2,
    v3,
    damp,
    l1,
    l2,
    s0,
    s1,
    s2,
    s3,
    mask,
    lhs,
    rhs,
    gsend,
    grecv,
    grad,
    rsend,
    rrecv,
    in_sem,
    hs,
    hr,
    ds,
    dr,
    f1s,
    f1r,
    f2s,
    f2r,
    gs,
    gr,
    rs,
    rr,
):
    naf, ngx, ngy, wx, wy, nz = sizes
    af, gx, gy = lax.axis_index("af"), lax.axis_index("gx"), lax.axis_index("gy")
    nx_ext = wx + 2 * HALO
    group = ngx * ngy

    loads = [pltpu.make_async_copy(pert, pertv, in_sem.at[0])]
    loads += [pltpu.make_async_copy(bg.at[0, p], bgv.at[p], in_sem.at[1 + p]) for p in range(2)]
    loads += [pltpu.make_async_copy(cond, condv, in_sem.at[3])]
    for load in loads:
        load.start()

    zeros = jnp.zeros((ROWS, nz), jnp.float32)
    for i in range(nx_ext):
        for k in range(3):
            damp[k, i] = zeros
        for p in range(2):
            for c in range(2):
                for k in range(3):
                    v0[p, c, k, i] = zeros
                for k in range(2):
                    l1[p, c, k, i] = zeros
                    l2[p, c, k, i] = zeros

    barrier = pltpu.get_barrier_semaphore()
    for step in range(1, group):
        pl.semaphore_signal(
            barrier,
            inc=1,
            device_id=(af, (gx + step // ngy) % ngx, (gy + step % ngy) % ngy),
            device_id_type=MESH,
        )
    for step in range(1, naf):
        pl.semaphore_signal(
            barrier, inc=1, device_id=((af + step) % naf, gx, gy), device_id_type=MESH
        )

    coupled = coup[0]
    loads[0].wait()
    weighted = [[coupled * pertv[k, i] for i in range(wx)] for k in range(3)]
    for p in range(2):
        loads[1 + p].wait()
        for k in range(3):
            for i in range(wx):
                v0[p, 0, k, X0 + i, Y0 : Y0 + wy] = weighted[k][i] * bgv[p, 1, k, i]
                v0[p, 1, k, X0 + i, Y0 : Y0 + wy] = -(weighted[k][i] * bgv[p, 0, k, i])
    loads[3].wait()
    for k in range(3):
        for i in range(wx):
            damp[k, X0 + i, Y0 : Y0 + wy] = coupled * condv[k, i]

    pl.semaphore_wait(barrier, group - 1 + naf - 1)

    def blocks(table, source, target, ssem, rsem):
        found = []
        for n, (a, b, k0, k1, xa, xb, ya, yb) in enumerate(table):
            tx, ty = gx + a, gy + b
            fx, fy = gx - a, gy - b
            sends = (tx >= 0) & (tx < ngx) & (ty >= 0) & (ty < ngy)
            gets = (fx >= 0) & (fx < ngx) & (fy >= 0) & (fy < ngy)
            copy = pltpu.make_async_remote_copy(
                src_ref=source.at[
                    ...,
                    k0:k1,
                    xa + a * wx + X0 : xb + a * wx + X0,
                    ya + b * wy + Y0 : yb + b * wy + Y0,
                    :,
                ],
                dst_ref=target.at[..., k0:k1, xa + X0 : xb + X0, ya + Y0 : yb + Y0, :],
                send_sem=ssem.at[n],
                recv_sem=rsem.at[n],
                device_id=(af, (tx + ngx) % ngx, (ty + ngy) % ngy),
                device_id_type=MESH,
            )
            found.append((sends, gets, copy))
        return found

    def start(found):
        for sends, _, copy in found:
            pl.when(sends)(copy.start)

    def wait_recv(found):
        for _, gets, copy in found:
            pl.when(gets)(copy.wait_recv)

    def wait_send(found):
        for sends, _, copy in found:
            pl.when(sends)(copy.wait_send)

    halo_d = blocks(damping_table(wx, wy), damp, damp, ds, dr)
    halos = [
        blocks(halo_table(wx, wy), v0.at[p], v0.at[p], hs.at[p], hr.at[p]) for p in range(2)
    ]
    frames1 = [
        blocks(frame1_table(wx, wy), v1.at[p], l1.at[p], f1s.at[p], f1r.at[p]) for p in range(2)
    ]
    frames2 = [
        blocks(frame2_table(wx, wy), v2.at[p], l2.at[p], f2s.at[p], f2r.at[p]) for p in range(2)
    ]
    start(halos[0])
    start(halo_d)
    start(halos[1])

    place = rec[...]
    span_y = wy * ngy
    pos_x = place // (span_y * nz) - gx * wx + X0
    pos_y = place // nz % span_y - gy * wy + Y0
    pos_z = place % nz
    inside = (pos_x >= 0) & (pos_x < nx_ext) & (pos_y >= 0) & (pos_y < ROWS)
    flat = jnp.where(inside, pos_x * ROWS + pos_y, -1)
    row_ids = lax.broadcasted_iota(jnp.int32, (nx_ext * ROWS, nz), 0)
    z_ids = lax.broadcasted_iota(jnp.int32, (nz, nz), 0)
    chunks = place.shape[0]
    for t in range(chunks):
        span = slice(t * nz, (t + 1) * nz)
        hit = row_ids == jnp.broadcast_to(flat[t : t + 1], row_ids.shape)
        lhs[:, span] = jnp.where(hit, 1.0, 0.0).astype(jnp.bfloat16)
        weight = wts[t : t + 1]
        high = weight.astype(jnp.bfloat16).astype(jnp.float32)
        rest = weight - high
        middle = rest.astype(jnp.bfloat16).astype(jnp.float32)
        low = rest - middle
        hit = z_ids == jnp.broadcast_to(pos_z[t : t + 1], z_ids.shape)
        for n, piece in enumerate((high, middle, low)):
            picked = jnp.where(hit, jnp.broadcast_to(piece, z_ids.shape), 0.0)
            rhs[n * nz : (n + 1) * nz, span] = picked.astype(jnp.bfloat16)
    found = lax.dot_general(
        lhs[...], rhs[...], (((1,), (1,)), ((), ())), preferred_element_type=jnp.float32
    )
    mask[...] = (found[:, :nz] + found[:, nz : 2 * nz] + found[:, 2 * nz :]).reshape(
        nx_ext, ROWS, nz
    )

    lane = lax.broadcasted_iota(jnp.int32, (ROWS, nz), 1)
    row = lax.broadcasted_iota(jnp.int32, (ROWS, nz), 0)
    first_lane, last_lane = lane == 0, lane == nz - 1
    grid_y = row - Y0 + gy * wy
    in_y = (grid_y >= 0) & (grid_y < ngy * wy)
    row_keep = jnp.where(in_y, 1.0, 0.0)

    def keep_of(i):
        grid_x = gx * wx + i - X0
        in_x = (grid_x >= 0) & (grid_x < ngx * wx)
        return row_keep * jnp.where(in_x, 1.0, 0.0)

    def z_up(f):
        return jnp.where(last_lane, 0.0, pltpu.roll(f, nz - 1, 1))

    def z_down(f):
        return jnp.where(first_lane, 0.0, pltpu.roll(f, 1, 1))

    def y_up(f):
        return pltpu.roll(f, ROWS - 1, 0)

    def y_down(f):
        return pltpu.roll(f, 1, 0)

    def faces(src, p, c, i):
        ex, ey, ez = (src[p, c, k, i] for k in range(3))
        next_y, next_z = src[p, c, 1, i + 1], src[p, c, 2, i + 1]
        face_y = (z_up(ex) - ex) - (next_z - ez)
        face_z = (next_y - ey) - (y_up(ex) - ex)
        face_x = (y_up(ez) - ez) - (z_up(ey) - ey)
        return face_x, face_y, face_z

    def apply(src, dst, p, low, high, bounded):
        before = [faces(src, p, c, low - 1)[1:] for c in range(2)]
        for i in range(low, high):
            keep = keep_of(i) if bounded else None
            curls = []
            for c in range(2):
                face_x, face_y, face_z = faces(src, p, c, i)
                old_y, old_z = before[c]
                curls.append(
                    (
                        (z_down(face_y) - face_y) - (y_down(face_z) - face_z),
                        (old_z - face_z) - (z_down(face_x) - face_x),
                        (y_down(face_x) - face_x) - (old_y - face_y),
                    )
                )
                before[c] = (face_y, face_z)
            for k in range(3):
                real, imag, d = src[p, 0, k, i], src[p, 1, k, i], damp[k, i]
                new_real = curls[0][k] - d * imag - real
                new_imag = curls[1][k] + d * real - imag
                if bounded:
                    new_real, new_imag = keep * new_real, keep * new_imag
                dst[p, 0, k, i] = new_real
                dst[p, 1, k, i] = new_imag

    lane8 = lax.broadcasted_iota(jnp.int32, (8, nz), 1)
    me = gx * ngy + gy

    def partial_gram(bufs, p, which):
        sums = {}
        for k in range(3):
            for i in range(X0, X0 + wx):
                parts = [
                    (b[p, 0, k, i, Y0 : Y0 + wy], b[p, 1, k, i, Y0 : Y0 + wy]) for b in bufs
                ]
                for j in range(4):
                    jr, ji = parts[j]
                    for l in range(j + 1):
                        lr, li = parts[l]
                        terms = [jr * lr + ji * li]
                        if l != j:
                            terms.append(jr * li - ji * lr)
                        for n, term in enumerate(terms):
                            key = (j, l, n)
                            sums[key] = term if key not in sums else sums[key] + term
        placed = jnp.zeros((8, nz), jnp.float32)
        for n, key in enumerate(sorted(sums)):
            placed = jnp.where(lane8 == n, jnp.sum(sums[key], axis=1, keepdims=True), placed)
        own = jnp.sum(placed, axis=0, keepdims=True)
        gsend[which, p] = own
        grecv[which, p, me] = own
        for step in range(1, group):
            pltpu.make_async_remote_copy(
                src_ref=gsend.at[which, p],
                dst_ref=grecv.at[which, p, me],
                send_sem=gs.at[which, p],
                recv_sem=gr.at[which, p],
                device_id=(af, (gx + step // ngy) % ngx, (gy + step % ngy) % ngy),
                device_id_type=MESH,
            ).start()

    def gram_wait(which, p):
        part = grecv.at[which, p, pl.ds(0, group - 1)]
        return pltpu.make_async_copy(part, part, gr.at[which, p]), pltpu.make_async_copy(
            part, part, gs.at[which, p]
        )

    def coefficients(which, p):
        gram_wait(which, p)[0].wait()
        total = grecv[which, p, 0]
        for n in range(1, group):
            total = total + grecv[which, p, n]
        names = []
        for j in range(4):
            for l in range(j + 1):
                names += [(j, l, 0)] if l == j else [(j, l, 0), (j, l, 1)]
        value = {
            key: jnp.broadcast_to(total[:, n : n + 1], (1, nz)) for n, key in enumerate(names)
        }
        gram = {}
        for j in range(4):
            for l in range(j + 1):
                if l == j:
                    gram[j, j] = (value[j, j, 0], jnp.zeros_like(value[j, j, 0]))
                else:
                    gram[j, l] = (value[j, l, 0], value[j, l, 1])
                    gram[l, j] = conj(gram[j, l])
        return solve_coefficients(gram, [relax[which, k] for k in range(3)])

    for p in range(2):
        wait_recv(halos[p])
        if p == 0:
            wait_recv(halo_d)
        apply(v0, v1, p, X0 - 2, X0 + wx + 2, True)
        start(frames1[p])
        apply(v1, v2, p, X0 - 1, X0 + wx + 1, True)
        start(frames2[p])
        apply(v2, v3, p, X0, X0 + wx, False)
        partial_gram((v0, v1, v2, v3), p, 0)

    for p in range(2):
        weights = coefficients(0, p)
        wait_recv(frames1[p])
        wait_recv(frames2[p])
        wide = [tuple(jnp.broadcast_to(v, (ROWS, nz)) for v in w) for w in weights]
        for i in range(nx_ext):
            station = mask[i]
            x = i - X0
            local_y = row - Y0
            in1 = (local_y >= -2) & (local_y < wy + 2)
            in2 = (local_y >= -1) & (local_y < wy + 1)
            for k in range(2):
                fields = [(v0[p, 0, k, i], v0[p, 1, k, i])]
                for buf, land, inner, width in ((v1, l1, in1, 2), (v2, l2, in2, 1)):
                    if -width <= x < wx + width:
                        fields.append(
                            tuple(
                                jnp.where(inner, buf[p, c, k, i], land[p, c, k, i])
                                for c in range(2)
                            )
                        )
                    else:
                        fields.append((land[p, 0, k, i], land[p, 1, k, i]))
                x_field = cmul(wide[0], fields[0])
                for n in (1, 2):
                    x_field = cadd(x_field, cmul(wide[n], fields[n]))
                s0[p, 0, k, i] = x_field[0] * station
                s0[p, 1, k, i] = x_field[1] * station
            s0[p, 0, 2, i] = zeros
            s0[p, 1, 2, i] = zeros
        apply(s0, s1, p, X0 - 2, X0 + wx + 2, True)
        apply(s1, s2, p, X0 - 1, X0 + wx + 1, True)
        apply(s2, s3, p, X0, X0 + wx, False)
        partial_gram((s0, s1, s2, s3), p, 1)

    grad[3 * wx * wy :] = jnp.zeros((nz - 3 * wx * wy, nz), jnp.float32)
    for p in range(2):
        weights = coefficients(1, p)
        wide = [tuple(jnp.broadcast_to(v, (wy, nz)) for v in w) for w in weights]
        for k in range(3):
            for i in range(wx):
                answer = None
                for n, buf in enumerate((s0, s1, s2)):
                    field = tuple(
                        buf[p, c, k, X0 + i, Y0 : Y0 + wy] for c in range(2)
                    )
                    term = cmul(wide[n], field)
                    answer = term if answer is None else cadd(answer, term)
                product = coupled * (
                    bgv[p, 0, k, i] * answer[1] + bgv[p, 1, k, i] * answer[0]
                )
                at = slice((k * wx + i) * wy, (k * wx + i + 1) * wy)
                grad[at] = product if p == 0 else grad[at] + product

    turned = grad[...].T
    depth = nz // naf
    for n in range(naf):
        rsend[n] = turned[n * depth : (n + 1) * depth]
    for step in range(1, naf):
        to = (af + step) % naf
        pltpu.make_async_remote_copy(
            src_ref=rsend.at[to],
            dst_ref=rrecv.at[af],
            send_sem=rs.at[0],
            recv_sem=rr.at[0],
            device_id=(to, gx, gy),
            device_id_type=MESH,
        ).start()
    rrecv[af] = rsend[af]

    wait_send(halo_d)
    for p in range(2):
        wait_send(halos[p])
        wait_send(frames1[p])
        wait_send(frames2[p])
        for which in range(2):
            gram_wait(which, p)[1].wait()

    part = rrecv.at[pl.ds(0, naf - 1)]
    pltpu.make_async_copy(part, part, rr.at[0]).wait()
    total = rrecv[0]
    for n in range(1, naf):
        total = total + rrecv[n]
    for n in range(3 * wx):
        out[n] = total[:, n * wy : (n + 1) * wy]
    pltpu.make_async_copy(part, part, rs.at[0]).wait()


def per_device(background, conductivity, perturbation, coupling, relaxation, receivers, weights):
    naf, ngx, ngy = lax.axis_size("af"), lax.axis_size("gx"), lax.axis_size("gy")
    wx, wy, nz = background.shape[4:]
    nx_ext = wx + 2 * HALO
    stations = receivers.shape[0]
    depth = nz // naf
    extended = pltpu.VMEM((2, 2, 3, nx_ext, ROWS, nz), jnp.float32)
    landing = pltpu.VMEM((2, 2, 2, nx_ext, ROWS, nz), jnp.float32)
    dma = pltpu.SemaphoreType.DMA
    smem = pl.BlockSpec(memory_space=pltpu.SMEM)
    vmem = pl.BlockSpec(memory_space=pltpu.VMEM)
    anyw = pl.BlockSpec(memory_space=pl.ANY)
    group = ngx * ngy
    result = pl.pallas_call(
        functools.partial(kernel, (naf, ngx, ngy, wx, wy, nz)),
        out_shape=jax.ShapeDtypeStruct((3 * wx, depth, wy), jnp.float32),
        in_specs=[anyw, anyw, anyw, smem, smem, vmem, vmem],
        out_specs=vmem,
        scratch_shapes=[
            pltpu.VMEM((2, 2, 3, wx, wy, nz), jnp.float32),
            pltpu.VMEM((3, wx, wy, nz), jnp.float32),
            pltpu.VMEM((3, wx, wy, nz), jnp.float32),
            extended,
            extended,
            extended,
            extended,
            pltpu.VMEM((3, nx_ext, ROWS, nz), jnp.float32),
            landing,
            landing,
            extended,
            extended,
            extended,
            extended,
            pltpu.VMEM((nx_ext, ROWS, nz), jnp.float32),
            pltpu.VMEM((nx_ext * ROWS, stations), jnp.bfloat16),
            pltpu.VMEM((3 * nz, stations), jnp.bfloat16),
            pltpu.VMEM((2, 2, 1, nz), jnp.float32),
            pltpu.VMEM((2, 2, group, 1, nz), jnp.float32),
            pltpu.VMEM((nz, nz), jnp.float32),
            pltpu.VMEM((naf, depth, nz), jnp.float32),
            pltpu.VMEM((naf, depth, nz), jnp.float32),
            dma((4,)),
            dma((2, 8)),
            dma((2, 8)),
            dma((8,)),
            dma((8,)),
            dma((2, 6)),
            dma((2, 6)),
            dma((2, 8)),
            dma((2, 8)),
            dma((2, 2)),
            dma((2, 2)),
            dma((1,)),
            dma((1,)),
        ],
        compiler_params=pltpu.CompilerParams(
            collective_id=0, has_side_effects=True, vmem_limit_bytes=40 * 1024 * 1024
        ),
    )(
        background,
        conductivity,
        perturbation,
        coupling,
        relaxation,
        receivers.reshape(stations // nz, nz),
        weights.reshape(stations // nz, nz),
    )
    return result.reshape(3, wx, depth, wy).transpose(0, 1, 3, 2)


def solution(mesh):
    placed = (
        P("af", None, None, None, "gx", "gy", None),
        P(None, "gx", "gy", None),
        P(None, "gx", "gy", None),
        P("af"),
        P(),
        P(),
        P("af", None),
    )
    return jax.shard_map(
        per_device, mesh=mesh, in_specs=placed, out_specs=P(None, "gx", "gy", "af"), check_vma=False
    )
```

time: 536 us -> 52.3 us (0.10); the launches traced: 528 us -> 52 us
  blocking collectives: 431 us -> 0 us
  starting transfers between devices: 53.6 us -> 0 us
  Pallas kernels: 0 us -> 46.8 us
  waiting for transfers between devices: 21.2 us -> 0 us
  other arithmetic: 15.3 us -> 0 us
    unnamed x1 -> x0, blocking collectives: 230 us -> none
    psum x6 -> x0, blocking collectives: 201 us -> none  [inner_sums(): return lax.psum((dot_real, dot_imag, squares), ('gx', 'gy'))]
    ppermute x24 -> x0, starting transfers between devices: 53.6 us -> none  [the longest x12 38.1 us: extended_2(): lax.ppermute(lax.slice_in_dim(block, block.shape[dim] - width, None, axis...]
    pallas_call x0 -> x1, Pallas kernels: none -> 46.8 us  [per_device(): pl.pallas_call(functools.partial(kernel, (naf, ngx, ngy, wx, wy, nz)), ou...]
    ppermute x24 -> x0, waiting for transfers between devices: 21.2 us -> none  [the longest x12 14.4 us: extended_2(): lax.ppermute(lax.slice_in_dim(block, 0, width, axis=dim), axis, backward)]
    scatter-add x1 -> x0, other arithmetic: 6.08 us -> none  [station_cells(): station_weight = jnp.zeros((weights.shape[0], cell_count), jnp.float32).a...]
  transfers between devices with their start and end apart: 24 -> 0, of which waited for: 11 -> 0; matrix products, arithmetic and copies ran while one was open for 2% -> 0% of each run, Pallas kernels for 0% -> 0%
where the time goes in v1:
time: 52.3 us; the launch traced here: 52 us
  Pallas kernels  46.8 us (89%)
  local copies, waits for them, and re-layouts  4.49 us (9%)
  between operations  0.69 us (1%)
    pallas_call x1, Pallas kernels, per_device(): pl.pallas_call(functools.partial(kernel, (naf, ngx, ngy, wx, wy, nz)), ou...  46.8 us
    unnamed x13, local copies, waits for them, and re-layouts  4.49 us

profile of v1, /device:TPU:1, one launch (start us, length us, event | category | flops | bytes accessed | tf_op | source)
XLA Modules:
  0.0 52.0 jit_solution(12832227501243946814)
XLA Ops:
  0.0 0.0 copy-start.3
  0.7 0.0 copy-start.5
  0.7 0.0 copy-done.3
  0.7 0.7 %copy-done.5 = f32[2,3]{1,0:T(2,128)S(1)} copy-done((f32[2,3]{1,0:T(2,128)S(1)}, f32[2,3]{1,0:T(2,128)}, u32[]{:S(2)}) %copy-start.5) | copy-done | bytes 48
  1.3 0.0 copy-start
  1.4 0.9 %copy-done = f32[1,2,2,3,4,8,128]{6,5,4,3,2,1,0:T(8,128)S(1)} copy-done((f32[1,2,2,3,4,8,128]{6,5,4,3,2,1,0:T(8,128)S(1)}, f32[1,2,2,3,4,8,128]{6,5,4,3,2,1,0:T(8,128)}, u32[]{:S(2)}) %copy-start) | copy-done | bytes 196632
  2.3 0.0 copy-start.1
  2.3 0.8 %copy-done.1 = f32[3,4,8,128]{3,2,1,0:T(8,128)S(1)} copy-done((f32[3,4,8,128]{3,2,1,0:T(8,128)S(1)}, f32[3,4,8,128]{3,2,1,0:T(8,128)}, u32[]{:S(2)}) %copy-start.1) | copy-done | bytes 49176
  3.1 0.0 copy-start.2
  3.1 0.8 %copy-done.2 = f32[3,4,8,128]{3,2,1,0:T(8,128)S(1)} copy-done((f32[3,4,8,128]{3,2,1,0:T(8,128)S(1)}, f32[3,4,8,128]{3,2,1,0:T(8,128)}, u32[]{:S(2)}) %copy-start.2) | copy-done | bytes 49176
  3.9 0.0 copy-start.4
  3.9 0.7 %copy-done.4 = f32[1,1024]{1,0:T(1,128)S(1)} copy-done((f32[1,1024]{1,0:T(1,128)S(1)}, f32[1,1024]{1,0:T(1,128)}, u32[]{:S(2)}) %copy-start.4) | copy-done | bytes 4120
  4.6 46.8 %shard_map.73 = f32[12,4,8]{2,1,0:T(4,128)S(1)} custom-call(f32[1,2,2,3,4,8,128]{6,5,4,3,2,1,0:T(8,128)S(1)} %copy-done, f32[3,4,8,128]{3,2,1,0:T(8,128)S(1)} %copy-done.1, f32[3,4,8,128]{3,2,1,0:T(8,128)S(1)} %copy-done.2, f32[1]{0:T(128)S(6)} %copy.9.coup, f32[2,3]{1,0:T(2,128)S(1)} %copy-done.5, s32[8,128]{1,0:T(8,128)S(1)} %bitcast.6, f32[8,128]{1,0:T(8,128)S(1)} %bitcast.7), custom_call_target="tpu_custom_call" | custom-call | tf_op jit(solution)/shard_map/pallas_call | solution.py:534
  51.4 0.6 %copy.10 = f32[3,4,8,4]{2,3,1,0:T(4,128)} copy(f32[3,4,8,4]{2,3,1,0:T(4,128)S(1)} %bitcast.5) | data formatting | bytes 3072
Async XLA Ops:
  0.0 0.7 %copy-start.3 = (s32[1024]{0:T(1024)S(1)}, s32[1024]{0:T(1024)}, u32[]{:S(2)}) copy-start(s32[1024]{0:T(1024)} %param.12) | copy-start | bytes 12292
  0.7 0.7 %copy-start.5 = (f32[2,3]{1,0:T(2,128)S(1)}, f32[2,3]{1,0:T(2,128)}, u32[]{:S(2)}) copy-start(f32[2,3]{1,0:T(2,128)} %relax.1) | copy-start | bytes 76
  1.3 0.9 %copy-start = (f32[1,2,2,3,4,8,128]{6,5,4,3,2,1,0:T(8,128)S(1)}, f32[1,2,2,3,4,8,128]{6,5,4,3,2,1,0:T(8,128)}, u32[]{:S(2)}) copy-start(f32[1,2,2,3,4,8,128]{6,5,4,3,2,1,0:T(8,128)} %bg.1) | copy-start | bytes 589828
  2.3 0.8 %copy-start.1 = (f32[3,4,8,128]{3,2,1,0:T(8,128)S(1)}, f32[3,4,8,128]{3,2,1,0:T(8,128)}, u32[]{:S(2)}) copy-start(f32[3,4,8,128]{3,2,1,0:T(8,128)} %cond.1) | copy-start | bytes 147460
  3.1 0.8 %copy-start.2 = (f32[3,4,8,128]{3,2,1,0:T(8,128)S(1)}, f32[3,4,8,128]{3,2,1,0:T(8,128)}, u32[]{:S(2)}) copy-start(f32[3,4,8,128]{3,2,1,0:T(8,128)} %pert.1) | copy-start | bytes 147460
  3.9 0.7 %copy-start.4 = (f32[1,1024]{1,0:T(1,128)S(1)}, f32[1,1024]{1,0:T(1,128)}, u32[]{:S(2)}) copy-start(f32[1,1024]{1,0:T(1,128)} %param.13) | copy-start | bytes 12292

commit v2 on v1

--- a/solution.py
+++ b/solution.py
@@ -12,6 +12,8 @@
 X0 = 3
 Y0 = 4
 ROWS = 16
+CORES = 2
+STRIDE = 4
 
 
 def halo_table(wx, wy):
@@ -40,28 +42,28 @@
     )
 
 
-def frame1_table(wx, wy):
+def frame_table(wx, wy):
     return (
-        (1, 0, 0, 2, -3, -2, 0, wy),
-        (-1, 0, 1, 2, wx + 2, wx + 3, 0, wy),
-        (0, 1, 0, 2, 0, wx, -3, -2),
-        (0, -1, 0, 1, 0, wx, wy + 2, wy + 3),
-        (1, -1, 0, 1, -3, 0, wy, wy + 3),
-        (-1, 1, 1, 2, wx, wx + 3, -3, 0),
-    )
-
-
-def frame2_table(wx, wy):
-    return (
-        (1, 0, 0, 2, -3, -1, 0, wy),
-        (-1, 0, 0, 2, wx + 1, wx + 3, 0, wy),
-        (0, 1, 0, 2, 0, wx, -3, -1),
-        (0, -1, 0, 2, 0, wx, wy + 1, wy + 3),
-        (1, 1, 0, 2, -2, 0, -2, 0),
-        (-1, -1, 0, 2, wx, wx + 2, wy, wy + 2),
-        (1, -1, 0, 2, -3, 0, wy, wy + 3),
-        (-1, 1, 0, 2, wx, wx + 3, -3, 0),
-    )
+        (0, 2, (1, 0, 0, 2, -3, -1, 0, wy)),
+        (0, 2, (-1, 0, 0, 2, wx + 1, wx + 3, 0, wy)),
+        (0, 2, (0, 1, 0, 2, 0, wx, -3, -1)),
+        (0, 2, (0, -1, 0, 2, 0, wx, wy + 1, wy + 3)),
+        (1, 2, (1, 1, 0, 2, -2, 0, -2, 0)),
+        (1, 2, (-1, -1, 0, 2, wx, wx + 2, wy, wy + 2)),
+        (0, 2, (1, -1, 0, 2, -3, 0, wy, wy + 3)),
+        (0, 2, (-1, 1, 0, 2, wx, wx + 3, -3, 0)),
+    )
+
+
+class Layer:
+    def __init__(self, ref, index):
+        self.ref, self.index = ref, index
+
+    def __getitem__(self, at):
+        return self.ref[(at[0], self.index) + at[1:]]
+
+    def __setitem__(self, at, value):
+        self.ref[(at[0], self.index) + at[1:]] = value
 
 
 def cmul(a, b):
@@ -125,21 +127,23 @@
     bg,
     cond,
     pert,
+    coup_hbm,
+    relax_hbm,
+    rec_hbm,
+    wts_hbm,
+    out,
+    bgv,
+    condv,
+    pertv,
     coup,
     relax,
     rec,
     wts,
-    out,
-    bgv,
-    condv,
-    pertv,
     v0,
-    v1,
-    v2,
+    v12,
     v3,
     damp,
-    l1,
-    l2,
+    land,
     s0,
     s1,
     s2,
@@ -147,76 +151,110 @@
     mask,
     lhs,
     rhs,
-    gsend,
-    grecv,
+    send_a,
+    recv_a,
+    send_b,
+    recv_b,
     grad,
     rsend,
-    rrecv,
+    rfirst,
+    rmid,
+    rlast,
     in_sem,
     hs,
     hr,
     ds,
     dr,
-    f1s,
-    f1r,
-    f2s,
-    f2r,
-    gs,
-    gr,
+    fs,
+    fr,
+    gas,
+    gar,
+    gbs,
+    gbr,
     rs,
     rr,
 ):
     naf, ngx, ngy, wx, wy, nz = sizes
     af, gx, gy = lax.axis_index("af"), lax.axis_index("gx"), lax.axis_index("gy")
     nx_ext = wx + 2 * HALO
-    group = ngx * ngy
-
-    loads = [pltpu.make_async_copy(pert, pertv, in_sem.at[0])]
-    loads += [pltpu.make_async_copy(bg.at[0, p], bgv.at[p], in_sem.at[1 + p]) for p in range(2)]
-    loads += [pltpu.make_async_copy(cond, condv, in_sem.at[3])]
+    nspan = naf // (CORES * STRIDE)
+    core, high, span = af % CORES, af // CORES % STRIDE, af // (CORES * STRIDE)
+    block_slot = span * CORES + core
+    nblock = naf // STRIDE
+    v1, v2 = Layer(v12, 0), Layer(v12, 1)
+
+    def af_of(a_span, a_high, a_core):
+        return (a_span * STRIDE + a_high) * CORES + a_core
+
+    loads = [
+        pltpu.make_async_copy(source, target, in_sem.at[n])
+        for n, (source, target) in enumerate(
+            (
+                (coup_hbm, coup),
+                (pert, pertv),
+                (bg.at[0, 0], bgv.at[0]),
+                (bg.at[0, 1], bgv.at[1]),
+                (cond, condv),
+                (relax_hbm, relax),
+                (rec_hbm, rec),
+                (wts_hbm, wts),
+            )
+        )
+    ]
     for load in loads:
         load.start()
 
     zeros = jnp.zeros((ROWS, nz), jnp.float32)
     for i in range(nx_ext):
-        for k in range(3):
-            damp[k, i] = zeros
         for p in range(2):
             for c in range(2):
                 for k in range(3):
                     v0[p, c, k, i] = zeros
-                for k in range(2):
-                    l1[p, c, k, i] = zeros
-                    l2[p, c, k, i] = zeros
 
     barrier = pltpu.get_barrier_semaphore()
-    for step in range(1, group):
-        pl.semaphore_signal(
-            barrier,
-            inc=1,
-            device_id=(af, (gx + step // ngy) % ngx, (gy + step % ngy) % ngy),
-            device_id_type=MESH,
-        )
-    for step in range(1, naf):
-        pl.semaphore_signal(
-            barrier, inc=1, device_id=((af + step) % naf, gx, gy), device_id_type=MESH
-        )
-
+
+    def greet(device):
+        pl.semaphore_signal(barrier, inc=1, device_id=device, device_id_type=MESH)
+
+    corners = [
+        ((tx >= 0) & (tx < ngx) & (ty >= 0) & (ty < ngy), tx, ty)
+        for tx, ty in ((gx - 1, gy - 1), (gx - 1, gy + 1), (gx + 1, gy - 1), (gx + 1, gy + 1))
+    ]
+    met = ngx - 1 + ngy - 1 + nblock - 1 + STRIDE - 1
+    for step in range(1, ngy):
+        greet((af, gx, (gy + step) % ngy))
+    for step in range(1, ngx):
+        greet((af, (gx + step) % ngx, gy))
+    for there, tx, ty in corners:
+        pl.when(there)(functools.partial(greet, (af, (tx + ngx) % ngx, (ty + ngy) % ngy)))
+        met = met + jnp.where(there, 1, 0)
+    block_peers = []
+    for step in range(1, nblock):
+        slot = (block_slot + step) % nblock
+        block_peers.append((slot, (af_of(slot // CORES, high, slot % CORES), gx, gy)))
+    high_peers = []
+    for step in range(1, STRIDE):
+        to = (high + step) % STRIDE
+        high_peers.append((to, (af_of(span, to, core), gx, gy)))
+    for _, device in block_peers + high_peers:
+        greet(device)
+
+    loads[0].wait()
     coupled = coup[0]
-    loads[0].wait()
+    loads[1].wait()
     weighted = [[coupled * pertv[k, i] for i in range(wx)] for k in range(3)]
     for p in range(2):
-        loads[1 + p].wait()
+        loads[2 + p].wait()
         for k in range(3):
             for i in range(wx):
                 v0[p, 0, k, X0 + i, Y0 : Y0 + wy] = weighted[k][i] * bgv[p, 1, k, i]
                 v0[p, 1, k, X0 + i, Y0 : Y0 + wy] = -(weighted[k][i] * bgv[p, 0, k, i])
-    loads[3].wait()
+    loads[4].wait()
     for k in range(3):
         for i in range(wx):
             damp[k, X0 + i, Y0 : Y0 + wy] = coupled * condv[k, i]
 
-    pl.semaphore_wait(barrier, group - 1 + naf - 1)
+    pl.semaphore_wait(barrier, met)
 
     def blocks(table, source, target, ssem, rsem):
         found = []
@@ -258,15 +296,24 @@
     halos = [
         blocks(halo_table(wx, wy), v0.at[p], v0.at[p], hs.at[p], hr.at[p]) for p in range(2)
     ]
-    frames1 = [
-        blocks(frame1_table(wx, wy), v1.at[p], l1.at[p], f1s.at[p], f1r.at[p]) for p in range(2)
-    ]
-    frames2 = [
-        blocks(frame2_table(wx, wy), v2.at[p], l2.at[p], f2s.at[p], f2r.at[p]) for p in range(2)
-    ]
+    frames = []
+    for p in range(2):
+        found = []
+        for n, (va, vb, entry) in enumerate(frame_table(wx, wy)):
+            found += blocks(
+                (entry,),
+                v12.at[p, va:vb],
+                land.at[p, va:vb],
+                fs.at[p, pl.ds(n, 1)],
+                fr.at[p, pl.ds(n, 1)],
+            )
+        frames.append(found)
     start(halos[0])
     start(halo_d)
     start(halos[1])
+
+    for load in loads[5:]:
+        load.wait()
 
     place = rec[...]
     span_y = wy * ngy
@@ -283,12 +330,12 @@
         hit = row_ids == jnp.broadcast_to(flat[t : t + 1], row_ids.shape)
         lhs[:, span] = jnp.where(hit, 1.0, 0.0).astype(jnp.bfloat16)
         weight = wts[t : t + 1]
-        high = weight.astype(jnp.bfloat16).astype(jnp.float32)
-        rest = weight - high
+        top = weight.astype(jnp.bfloat16).astype(jnp.float32)
+        rest = weight - top
         middle = rest.astype(jnp.bfloat16).astype(jnp.float32)
         low = rest - middle
         hit = z_ids == jnp.broadcast_to(pos_z[t : t + 1], z_ids.shape)
-        for n, piece in enumerate((high, middle, low)):
+        for n, piece in enumerate((top, middle, low)):
             picked = jnp.where(hit, jnp.broadcast_to(piece, z_ids.shape), 0.0)
             rhs[n * nz : (n + 1) * nz, span] = picked.astype(jnp.bfloat16)
     found = lax.dot_general(
@@ -302,13 +349,10 @@
     row = lax.broadcasted_iota(jnp.int32, (ROWS, nz), 0)
     first_lane, last_lane = lane == 0, lane == nz - 1
     grid_y = row - Y0 + gy * wy
-    in_y = (grid_y >= 0) & (grid_y < ngy * wy)
-    row_keep = jnp.where(in_y, 1.0, 0.0)
 
     def keep_of(i):
-        grid_x = gx * wx + i - X0
-        in_x = (grid_x >= 0) & (grid_x < ngx * wx)
-        return row_keep * jnp.where(in_x, 1.0, 0.0)
+        shift = jnp.where((gx * wx + i - X0 >= 0) & (gx * wx + i - X0 < ngx * wx), 0, ngy * wy)
+        return (grid_y >= shift) & (grid_y < ngy * wy)
 
     def z_up(f):
         return jnp.where(last_lane, 0.0, pltpu.roll(f, nz - 1, 1))
@@ -351,12 +395,12 @@
                 new_real = curls[0][k] - d * imag - real
                 new_imag = curls[1][k] + d * real - imag
                 if bounded:
-                    new_real, new_imag = keep * new_real, keep * new_imag
+                    new_real = jnp.where(keep, new_real, 0.0)
+                    new_imag = jnp.where(keep, new_imag, 0.0)
                 dst[p, 0, k, i] = new_real
                 dst[p, 1, k, i] = new_imag
 
     lane8 = lax.broadcasted_iota(jnp.int32, (8, nz), 1)
-    me = gx * ngy + gy
 
     def partial_gram(bufs, p, which):
         sums = {}
@@ -379,29 +423,44 @@
         for n, key in enumerate(sorted(sums)):
             placed = jnp.where(lane8 == n, jnp.sum(sums[key], axis=1, keepdims=True), placed)
         own = jnp.sum(placed, axis=0, keepdims=True)
-        gsend[which, p] = own
-        grecv[which, p, me] = own
-        for step in range(1, group):
+        send_a[which, p] = own
+        recv_a[which, p, gy] = own
+        for step in range(1, ngy):
             pltpu.make_async_remote_copy(
-                src_ref=gsend.at[which, p],
-                dst_ref=grecv.at[which, p, me],
-                send_sem=gs.at[which, p],
-                recv_sem=gr.at[which, p],
-                device_id=(af, (gx + step // ngy) % ngx, (gy + step % ngy) % ngy),
+                src_ref=send_a.at[which, p],
+                dst_ref=recv_a.at[which, p, gy],
+                send_sem=gas.at[which, p],
+                recv_sem=gar.at[which, p],
+                device_id=(af, gx, (gy + step) % ngy),
                 device_id_type=MESH,
             ).start()
 
-    def gram_wait(which, p):
-        part = grecv.at[which, p, pl.ds(0, group - 1)]
-        return pltpu.make_async_copy(part, part, gr.at[which, p]), pltpu.make_async_copy(
-            part, part, gs.at[which, p]
-        )
+    def wait_for(ref, count, sem):
+        part = ref.at[pl.ds(0, count)]
+        pltpu.make_async_copy(part, part, sem).wait()
+
+    def pass_on(which, p):
+        wait_for(recv_a.at[which, p], ngy - 1, gar.at[which, p])
+        own = recv_a[which, p, 0]
+        for n in range(1, ngy):
+            own = own + recv_a[which, p, n]
+        send_b[which, p] = own
+        recv_b[which, p, gx] = own
+        for step in range(1, ngx):
+            pltpu.make_async_remote_copy(
+                src_ref=send_b.at[which, p],
+                dst_ref=recv_b.at[which, p, gx],
+                send_sem=gbs.at[which, p],
+                recv_sem=gbr.at[which, p],
+                device_id=(af, (gx + step) % ngx, gy),
+                device_id_type=MESH,
+            ).start()
 
     def coefficients(which, p):
-        gram_wait(which, p)[0].wait()
-        total = grecv[which, p, 0]
-        for n in range(1, group):
-            total = total + grecv[which, p, n]
+        wait_for(recv_b.at[which, p], ngx - 1, gbr.at[which, p])
+        total = recv_b[which, p, 0]
+        for n in range(1, ngx):
+            total = total + recv_b[which, p, n]
         names = []
         for j in range(4):
             for l in range(j + 1):
@@ -424,49 +483,53 @@
         if p == 0:
             wait_recv(halo_d)
         apply(v0, v1, p, X0 - 2, X0 + wx + 2, True)
-        start(frames1[p])
+        if p == 1:
+            pass_on(0, 0)
         apply(v1, v2, p, X0 - 1, X0 + wx + 1, True)
-        start(frames2[p])
+        start(frames[p])
         apply(v2, v3, p, X0, X0 + wx, False)
         partial_gram((v0, v1, v2, v3), p, 0)
 
     for p in range(2):
         weights = coefficients(0, p)
-        wait_recv(frames1[p])
-        wait_recv(frames2[p])
+        wait_recv(frames[p])
         wide = [tuple(jnp.broadcast_to(v, (ROWS, nz)) for v in w) for w in weights]
         for i in range(nx_ext):
             station = mask[i]
+            keep = keep_of(i)
             x = i - X0
             local_y = row - Y0
             in1 = (local_y >= -2) & (local_y < wy + 2)
             in2 = (local_y >= -1) & (local_y < wy + 1)
             for k in range(2):
                 fields = [(v0[p, 0, k, i], v0[p, 1, k, i])]
-                for buf, land, inner, width in ((v1, l1, in1, 2), (v2, l2, in2, 1)):
+                for buf, m, inner, width in ((v1, 0, in1, 2), (v2, 1, in2, 1)):
                     if -width <= x < wx + width:
                         fields.append(
                             tuple(
-                                jnp.where(inner, buf[p, c, k, i], land[p, c, k, i])
+                                jnp.where(inner, buf[p, c, k, i], land[p, m, c, k, i])
                                 for c in range(2)
                             )
                         )
                     else:
-                        fields.append((land[p, 0, k, i], land[p, 1, k, i]))
+                        fields.append((land[p, m, 0, k, i], land[p, m, 1, k, i]))
                 x_field = cmul(wide[0], fields[0])
                 for n in (1, 2):
                     x_field = cadd(x_field, cmul(wide[n], fields[n]))
-                s0[p, 0, k, i] = x_field[0] * station
-                s0[p, 1, k, i] = x_field[1] * station
+                s0[p, 0, k, i] = jnp.where(keep, x_field[0] * station, 0.0)
+                s0[p, 1, k, i] = jnp.where(keep, x_field[1] * station, 0.0)
             s0[p, 0, 2, i] = zeros
             s0[p, 1, 2, i] = zeros
         apply(s0, s1, p, X0 - 2, X0 + wx + 2, True)
+        pass_on(*((0, 1) if p == 0 else (1, 0)))
         apply(s1, s2, p, X0 - 1, X0 + wx + 1, True)
         apply(s2, s3, p, X0, X0 + wx, False)
         partial_gram((s0, s1, s2, s3), p, 1)
 
     grad[3 * wx * wy :] = jnp.zeros((nz - 3 * wx * wy, nz), jnp.float32)
     for p in range(2):
+        if p == 1:
+            pass_on(1, 1)
         weights = coefficients(1, p)
         wide = [tuple(jnp.broadcast_to(v, (wy, nz)) for v in w) for w in weights]
         for k in range(3):
@@ -486,36 +549,53 @@
 
     turned = grad[...].T
     depth = nz // naf
-    for n in range(naf):
-        rsend[n] = turned[n * depth : (n + 1) * depth]
-    for step in range(1, naf):
-        to = (af + step) % naf
+    for a_span in range(nspan):
+        for a_high in range(STRIDE):
+            for a_core in range(CORES):
+                n = af_of(a_span, a_high, a_core)
+                rsend[a_span * CORES + a_core, a_high] = turned[n * depth : (n + 1) * depth]
+    for slot, device in block_peers:
         pltpu.make_async_remote_copy(
-            src_ref=rsend.at[to],
-            dst_ref=rrecv.at[af],
+            src_ref=rsend.at[slot],
+            dst_ref=rfirst.at[block_slot],
             send_sem=rs.at[0],
             recv_sem=rr.at[0],
-            device_id=(to, gx, gy),
+            device_id=device,
             device_id_type=MESH,
         ).start()
-    rrecv[af] = rsend[af]
+    rfirst[block_slot] = rsend[block_slot]
 
     wait_send(halo_d)
     for p in range(2):
         wait_send(halos[p])
-        wait_send(frames1[p])
-        wait_send(frames2[p])
+        wait_send(frames[p])
         for which in range(2):
-            gram_wait(which, p)[1].wait()
-
-    part = rrecv.at[pl.ds(0, naf - 1)]
-    pltpu.make_async_copy(part, part, rr.at[0]).wait()
-    total = rrecv[0]
-    for n in range(1, naf):
-        total = total + rrecv[n]
+            wait_for(recv_a.at[which, p], ngy - 1, gas.at[which, p])
+            wait_for(recv_b.at[which, p], ngx - 1, gbs.at[which, p])
+
+    wait_for(rfirst, nblock - 1, rr.at[0])
+    total = rfirst[0]
+    for n in range(1, nblock):
+        total = total + rfirst[n]
+    rmid[...] = total
+    for to, device in high_peers:
+        pltpu.make_async_remote_copy(
+            src_ref=rmid.at[to],
+            dst_ref=rlast.at[high],
+            send_sem=rs.at[1],
+            recv_sem=rr.at[1],
+            device_id=device,
+            device_id_type=MESH,
+        ).start()
+    rlast[high] = rmid[high]
+    wait_for(rfirst, nblock - 1, rs.at[0])
+    wait_for(rlast, STRIDE - 1, rr.at[1])
+    total = rlast[0]
+    for n in range(1, STRIDE):
+        total = total + rlast[n]
     for n in range(3 * wx):
         out[n] = total[:, n * wy : (n + 1) * wy]
-    pltpu.make_async_copy(part, part, rs.at[0]).wait()
+    wait_for(rlast, STRIDE - 1, rs.at[1])
 
 
 def per_device(background, conductivity, perturbation, coupling, relaxation, receivers, weights):
@@ -524,29 +604,28 @@
     nx_ext = wx + 2 * HALO
     stations = receivers.shape[0]
     depth = nz // naf
+    nblock = naf // STRIDE
     extended = pltpu.VMEM((2, 2, 3, nx_ext, ROWS, nz), jnp.float32)
-    landing = pltpu.VMEM((2, 2, 2, nx_ext, ROWS, nz), jnp.float32)
     dma = pltpu.SemaphoreType.DMA
-    smem = pl.BlockSpec(memory_space=pltpu.SMEM)
-    vmem = pl.BlockSpec(memory_space=pltpu.VMEM)
-    anyw = pl.BlockSpec(memory_space=pl.ANY)
-    group = ngx * ngy
+    far = pl.BlockSpec(memory_space=pltpu.HBM)
     result = pl.pallas_call(
         functools.partial(kernel, (naf, ngx, ngy, wx, wy, nz)),
         out_shape=jax.ShapeDtypeStruct((3 * wx, depth, wy), jnp.float32),
-        in_specs=[anyw, anyw, anyw, smem, smem, vmem, vmem],
-        out_specs=vmem,
+        in_specs=[far] * 7,
+        out_specs=pl.BlockSpec(memory_space=pltpu.VMEM),
         scratch_shapes=[
             pltpu.VMEM((2, 2, 3, wx, wy, nz), jnp.float32),
             pltpu.VMEM((3, wx, wy, nz), jnp.float32),
             pltpu.VMEM((3, wx, wy, nz), jnp.float32),
+            pltpu.SMEM((1,), jnp.float32),
+            pltpu.SMEM((2, 3), jnp.float32),
+            pltpu.VMEM((stations // nz, nz), jnp.int32),
+            pltpu.VMEM((stations // nz, nz), jnp.float32),
             extended,
-            extended,
-            extended,
+            pltpu.VMEM((2, 2, 2, 3, nx_ext, ROWS, nz), jnp.float32),
             extended,
             pltpu.VMEM((3, nx_ext, ROWS, nz), jnp.float32),
-            landing,
-            landing,
+            pltpu.VMEM((2, 2, 2, 2, nx_ext, ROWS, nz), jnp.float32),
             extended,
             extended,
             extended,
@@ -555,26 +634,30 @@
             pltpu.VMEM((nx_ext * ROWS, stations), jnp.bfloat16),
             pltpu.VMEM((3 * nz, stations), jnp.bfloat16),
             pltpu.VMEM((2, 2, 1, nz), jnp.float32),
-            pltpu.VMEM((2, 2, group, 1, nz), jnp.float32),
+            pltpu.VMEM((2, 2, ngy, 1, nz), jnp.float32),
+            pltpu.VMEM((2, 2, 1, nz), jnp.float32),
+            pltpu.VMEM((2, 2, ngx, 1, nz), jnp.float32),
             pltpu.VMEM((nz, nz), jnp.float32),
-            pltpu.VMEM((naf, depth, nz), jnp.float32),
-            pltpu.VMEM((naf, depth, nz), jnp.float32),
-            dma((4,)),
+            pltpu.VMEM((nblock, STRIDE, depth, nz), jnp.float32),
+            pltpu.VMEM((nblock, STRIDE, depth, nz), jnp.float32),
+            pltpu.VMEM((STRIDE, depth, nz), jnp.float32),
+            pltpu.VMEM((STRIDE, depth, nz), jnp.float32),
+            dma((8,)),
             dma((2, 8)),
             dma((2, 8)),
             dma((8,)),
             dma((8,)),
-            dma((2, 6)),
-            dma((2, 6)),
             dma((2, 8)),
             dma((2, 8)),
             dma((2, 2)),
             dma((2, 2)),
-            dma((1,)),
-            dma((1,)),
+            dma((2, 2)),
+            dma((2, 2)),
+            dma((2,)),
+            dma((2,)),
         ],
         compiler_params=pltpu.CompilerParams(
-            collective_id=0, has_side_effects=True, vmem_limit_bytes=40 * 1024 * 1024
+            collective_id=0, has_side_effects=True, vmem_limit_bytes=62 * 1024 * 1024
         ),
     )(
         background,

time: 52.3 us -> 55.4 us (1.059)
  Pallas kernels: 46.8 us -> 53.2 us
  local copies, waits for them, and re-layouts: 4.49 us -> 1.35 us
    pallas_call x1, Pallas kernels: 46.8 us -> 53.2 us  [per_device(): pl.pallas_call(functools.partial(kernel, (naf, ngx, ngy, wx, wy, nz)), ou...]
    unnamed x13 -> x1, local copies, waits for them, and re-layouts: 4.49 us -> 1.35 us
where the time goes in v2:
time: 55.4 us; the launch traced here: 55.2 us
  Pallas kernels  53.2 us (96%)
  local copies, waits for them, and re-layouts  1.35 us (2%)
  between operations  0.66 us (1%)
    pallas_call x1, Pallas kernels, per_device(): pl.pallas_call(functools.partial(kernel, (naf, ngx, ngy, wx, wy, nz)), ou...  53.2 us
    unnamed x1, local copies, waits for them, and re-layouts  1.35 us

profile of v2, /device:TPU:1, one launch (start us, length us, event | category | flops | bytes accessed | tf_op | source)
XLA Modules:
  0.0 55.2 jit_solution(210722450744169879)
XLA Ops:
  0.7 53.2 %shard_map.73 = f32[12,4,8]{2,1,0:T(4,128)} custom-call(f32[1,2,2,3,4,8,128]{6,5,4,3,2,1,0:T(8,128)} %bg.1, f32[3,4,8,128]{3,2,1,0:T(8,128)} %cond.1, f32[3,4,8,128]{3,2,1,0:T(8,128)} %pert.1, f32[1]{0:T(128)S(6)} %copy.9.coup_hbm, f32[2,3]{1,0:T(2,128)} %relax_hbm.1, s32[8,128]{1,0:T(8,128)} %bitcast.6, f32[8,128]{1,0:T(8,128)} %bitcast.7), custom_call_target="tpu_custom_call" | custom-call | tf_op jit(solution)/shard_map/pallas_call | solution.py:611
  53.9 1.3 %copy.10 = f32[3,4,8,4]{2,3,1,0:T(4,128)} copy(f32[3,4,8,4]{2,3,1,0:T(4,128)} %bitcast.5) | data formatting | bytes 3072

commit v3 on v2

--- a/solution.py
+++ b/solution.py
@@ -19,13 +19,16 @@
 def halo_table(wx, wy):
     return (
         (1, 0, 0, 3, -3, 0, 0, wy),
-        (-1, 0, 0, 3, wx, wx + 3, 0, wy),
+        (-1, 0, 1, 3, wx, wx + 3, 0, wy),
+        (-1, 0, 0, 1, wx, wx + 2, 0, wy),
+        (1, 1, 0, 3, -2, 0, -2, 0),
+        (-1, -1, 0, 3, wx, wx + 2, wy, wy + 2),
+        (1, -1, 0, 1, -3, 0, wy, wy + 3),
+        (1, -1, 1, 3, -2, 0, wy, wy + 2),
+        (-1, 1, 0, 2, wx, wx + 3, -3, 0),
+        (-1, 1, 2, 3, wx, wx + 2, -2, 0),
         (0, 1, 0, 3, 0, wx, -3, 0),
         (0, -1, 0, 3, 0, wx, wy, wy + 3),
-        (1, 1, 0, 3, -2, 0, -2, 0),
-        (-1, -1, 0, 3, wx, wx + 2, wy, wy + 2),
-        (1, -1, 0, 3, -3, 0, wy, wy + 3),
-        (-1, 1, 0, 3, wx, wx + 3, -3, 0),
     )
 
 
@@ -33,25 +36,29 @@
     return (
         (1, 0, 0, 3, -2, 0, 0, wy),
         (-1, 0, 0, 3, wx, wx + 2, 0, wy),
-        (0, 1, 0, 3, 0, wx, -2, 0),
-        (0, -1, 0, 3, 0, wx, wy, wy + 2),
         (1, 1, 0, 3, -2, 0, -2, 0),
         (-1, -1, 0, 3, wx, wx + 2, wy, wy + 2),
         (1, -1, 0, 3, -2, 0, wy, wy + 2),
         (-1, 1, 0, 3, wx, wx + 2, -2, 0),
+        (0, 1, 0, 3, 0, wx, -2, 0),
+        (0, -1, 0, 3, 0, wx, wy, wy + 2),
     )
 
 
 def frame_table(wx, wy):
     return (
-        (0, 2, (1, 0, 0, 2, -3, -1, 0, wy)),
-        (0, 2, (-1, 0, 0, 2, wx + 1, wx + 3, 0, wy)),
+        (0, 1, (1, 0, 0, 2, -3, -2, 0, wy)),
+        (1, 2, (1, 0, 0, 2, -3, -1, 0, wy)),
+        (0, 1, (-1, 0, 1, 2, wx + 2, wx + 3, 0, wy)),
+        (1, 2, (-1, 0, 0, 2, wx + 1, wx + 3, 0, wy)),
+        (0, 2, (1, 1, 0, 2, -2, 0, -2, 0)),
+        (0, 2, (-1, -1, 0, 2, wx, wx + 2, wy, wy + 2)),
+        (0, 2, (1, -1, 0, 1, -3, 0, wy, wy + 3)),
+        (0, 2, (1, -1, 1, 2, -2, 0, wy, wy + 2)),
+        (0, 2, (-1, 1, 1, 2, wx, wx + 3, -3, 0)),
+        (0, 2, (-1, 1, 0, 1, wx, wx + 2, -2, 0)),
         (0, 2, (0, 1, 0, 2, 0, wx, -3, -1)),
         (0, 2, (0, -1, 0, 2, 0, wx, wy + 1, wy + 3)),
-        (1, 2, (1, 1, 0, 2, -2, 0, -2, 0)),
-        (1, 2, (-1, -1, 0, 2, wx, wx + 2, wy, wy + 2)),
-        (0, 2, (1, -1, 0, 2, -3, 0, wy, wy + 3)),
-        (0, 2, (-1, 1, 0, 2, wx, wx + 3, -3, 0)),
     )
 
 
@@ -153,8 +160,6 @@
     rhs,
     send_a,
     recv_a,
-    send_b,
-    recv_b,
     grad,
     rsend,
     rfirst,
@@ -169,8 +174,6 @@
     fr,
     gas,
     gar,
-    gbs,
-    gbr,
     rs,
     rr,
 ):
@@ -179,8 +182,8 @@
     nx_ext = wx + 2 * HALO
     nspan = naf // (CORES * STRIDE)
     core, high, span = af % CORES, af // CORES % STRIDE, af // (CORES * STRIDE)
-    block_slot = span * CORES + core
-    nblock = naf // STRIDE
+    nchip = nspan * STRIDE
+    chip = span * STRIDE + high
     v1, v2 = Layer(v12, 0), Layer(v12, 1)
 
     def af_of(a_span, a_high, a_core):
@@ -216,28 +219,28 @@
     def greet(device):
         pl.semaphore_signal(barrier, inc=1, device_id=device, device_id_type=MESH)
 
-    corners = [
-        ((tx >= 0) & (tx < ngx) & (ty >= 0) & (ty < ngy), tx, ty)
-        for tx, ty in ((gx - 1, gy - 1), (gx - 1, gy + 1), (gx + 1, gy - 1), (gx + 1, gy + 1))
+    group_peers = [
+        (af, gx ^ dx, gy ^ dy)
+        for dx, dy in sorted(
+            ((dx, dy) for dx in range(ngx) for dy in range(ngy) if dx or dy),
+            key=lambda d: (-d[0] - min(d[1], 2), d),
+        )
     ]
-    met = ngx - 1 + ngy - 1 + nblock - 1 + STRIDE - 1
-    for step in range(1, ngy):
-        greet((af, gx, (gy + step) % ngy))
-    for step in range(1, ngx):
-        greet((af, (gx + step) % ngx, gy))
-    for there, tx, ty in corners:
-        pl.when(there)(functools.partial(greet, (af, (tx + ngx) % ngx, (ty + ngy) % ngy)))
-        met = met + jnp.where(there, 1, 0)
-    block_peers = []
-    for step in range(1, nblock):
-        slot = (block_slot + step) % nblock
-        block_peers.append((slot, (af_of(slot // CORES, high, slot % CORES), gx, gy)))
-    high_peers = []
-    for step in range(1, STRIDE):
-        to = (high + step) % STRIDE
-        high_peers.append((to, (af_of(span, to, core), gx, gy)))
-    for _, device in block_peers + high_peers:
+    twin = (af_of(span, high, 1 - core), gx, gy)
+    far_peers = []
+    for d_high in (2, 1, 3, 0):
+        for d_span in (2, 1, 3, 0):
+            if d_high or d_span:
+                to_span, to_high = span ^ d_span, (high + d_high) % STRIDE
+                far_peers.append(
+                    (to_span * STRIDE + to_high, (af_of(to_span, to_high, core), gx, gy))
+                )
+    for _, device in far_peers:
         greet(device)
+    for device in group_peers:
+        greet(device)
+    greet(twin)
+    met = len(far_peers) + len(group_peers) + 1
 
     loads[0].wait()
     coupled = coup[0]
@@ -400,6 +403,8 @@
                 dst[p, 0, k, i] = new_real
                 dst[p, 1, k, i] = new_imag
 
+    group = ngx * ngy
+    me = gx * ngy + gy
     lane8 = lax.broadcasted_iota(jnp.int32, (8, nz), 1)
 
     def partial_gram(bufs, p, which):
@@ -424,14 +429,14 @@
             placed = jnp.where(lane8 == n, jnp.sum(sums[key], axis=1, keepdims=True), placed)
         own = jnp.sum(placed, axis=0, keepdims=True)
         send_a[which, p] = own
-        recv_a[which, p, gy] = own
-        for step in range(1, ngy):
+        recv_a[which, p, me] = own
+        for device in group_peers:
             pltpu.make_async_remote_copy(
                 src_ref=send_a.at[which, p],
-                dst_ref=recv_a.at[which, p, gy],
+                dst_ref=recv_a.at[which, p, me],
                 send_sem=gas.at[which, p],
                 recv_sem=gar.at[which, p],
-                device_id=(af, gx, (gy + step) % ngy),
+                device_id=device,
                 device_id_type=MESH,
             ).start()
 
@@ -439,28 +444,11 @@
         part = ref.at[pl.ds(0, count)]
         pltpu.make_async_copy(part, part, sem).wait()
 
-    def pass_on(which, p):
-        wait_for(recv_a.at[which, p], ngy - 1, gar.at[which, p])
-        own = recv_a[which, p, 0]
-        for n in range(1, ngy):
-            own = own + recv_a[which, p, n]
-        send_b[which, p] = own
-        recv_b[which, p, gx] = own
-        for step in range(1, ngx):
-            pltpu.make_async_remote_copy(
-                src_ref=send_b.at[which, p],
-                dst_ref=recv_b.at[which, p, gx],
-                send_sem=gbs.at[which, p],
-                recv_sem=gbr.at[which, p],
-                device_id=(af, (gx + step) % ngx, gy),
-                device_id_type=MESH,
-            ).start()
-
     def coefficients(which, p):
-        wait_for(recv_b.at[which, p], ngx - 1, gbr.at[which, p])
-        total = recv_b[which, p, 0]
-        for n in range(1, ngx):
-            total = total + recv_b[which, p, n]
+        wait_for(recv_a.at[which, p], group - 1, gar.at[which, p])
+        total = recv_a[which, p, 0]
+        for n in range(1, group):
+            total = total + recv_a[which, p, n]
         names = []
         for j in range(4):
             for l in range(j + 1):
@@ -483,12 +471,10 @@
         if p == 0:
             wait_recv(halo_d)
         apply(v0, v1, p, X0 - 2, X0 + wx + 2, True)
-        if p == 1:
-            pass_on(0, 0)
         apply(v1, v2, p, X0 - 1, X0 + wx + 1, True)
-        start(frames[p])
         apply(v2, v3, p, X0, X0 + wx, False)
         partial_gram((v0, v1, v2, v3), p, 0)
+        start(frames[p])
 
     for p in range(2):
         weights = coefficients(0, p)
@@ -499,15 +485,17 @@
             keep = keep_of(i)
             x = i - X0
             local_y = row - Y0
+            own_rows = (local_y >= 0) & (local_y < wy)
             in1 = (local_y >= -2) & (local_y < wy + 2)
             in2 = (local_y >= -1) & (local_y < wy + 1)
             for k in range(2):
                 fields = [(v0[p, 0, k, i], v0[p, 1, k, i])]
                 for buf, m, inner, width in ((v1, 0, in1, 2), (v2, 1, in2, 1)):
                     if -width <= x < wx + width:
+                        inside = inner if 0 <= x < wx else own_rows
                         fields.append(
                             tuple(
-                                jnp.where(inner, buf[p, c, k, i], land[p, m, c, k, i])
+                                jnp.where(inside, buf[p, c, k, i], land[p, m, c, k, i])
                                 for c in range(2)
                             )
                         )
@@ -521,15 +509,12 @@
             s0[p, 0, 2, i] = zeros
             s0[p, 1, 2, i] = zeros
         apply(s0, s1, p, X0 - 2, X0 + wx + 2, True)
-        pass_on(*((0, 1) if p == 0 else (1, 0)))
         apply(s1, s2, p, X0 - 1, X0 + wx + 1, True)
         apply(s2, s3, p, X0, X0 + wx, False)
         partial_gram((s0, s1, s2, s3), p, 1)
 
     grad[3 * wx * wy :] = jnp.zeros((nz - 3 * wx * wy, nz), jnp.float32)
     for p in range(2):
-        if p == 1:
-            pass_on(1, 1)
         weights = coefficients(1, p)
         wide = [tuple(jnp.broadcast_to(v, (wy, nz)) for v in w) for w in weights]
         for k in range(3):
@@ -549,53 +534,46 @@
 
     turned = grad[...].T
     depth = nz // naf
-    for a_span in range(nspan):
-        for a_high in range(STRIDE):
-            for a_core in range(CORES):
-                n = af_of(a_span, a_high, a_core)
-                rsend[a_span * CORES + a_core, a_high] = turned[n * depth : (n + 1) * depth]
-    for slot, device in block_peers:
-        pltpu.make_async_remote_copy(
-            src_ref=rsend.at[slot],
-            dst_ref=rfirst.at[block_slot],
-            send_sem=rs.at[0],
-            recv_sem=rr.at[0],
-            device_id=device,
-            device_id_type=MESH,
-        ).start()
-    rfirst[block_slot] = rsend[block_slot]
+    for a_core in range(CORES):
+        for n in range(nchip):
+            at = (n * CORES + a_core) * depth
+            rsend[a_core, n] = turned[at : at + depth]
+    swap = pltpu.make_async_remote_copy(
+        src_ref=rsend.at[1 - core],
+        dst_ref=rfirst,
+        send_sem=rs.at[0],
+        recv_sem=rr.at[0],
+        device_id=twin,
+        device_id_type=MESH,
+    )
+    swap.start()
 
     wait_send(halo_d)
     for p in range(2):
         wait_send(halos[p])
         wait_send(frames[p])
         for which in range(2):
-            wait_for(recv_a.at[which, p], ngy - 1, gas.at[which, p])
-            wait_for(recv_b.at[which, p], ngx - 1, gbs.at[which, p])
-
-    wait_for(rfirst, nblock - 1, rr.at[0])
-    total = rfirst[0]
-    for n in range(1, nblock):
-        total = total + rfirst[n]
-    rmid[...] = total
-    for to, device in high_peers:
+            wait_for(recv_a.at[which, p], group - 1, gas.at[which, p])
+
+    swap.wait()
+    rmid[...] = rsend[core] + rfirst[...]
+    for to, device in far_peers:
         pltpu.make_async_remote_copy(
             src_ref=rmid.at[to],
-            dst_ref=rlast.at[high],
+            dst_ref=rlast.at[chip],
             send_sem=rs.at[1],
             recv_sem=rr.at[1],
             device_id=device,
             device_id_type=MESH,
         ).start()
-    rlast[high] = rmid[high]
-    wait_for(rfirst, nblock - 1, rs.at[0])
-    wait_for(rlast, STRIDE - 1, rr.at[1])
+    rlast[chip] = rmid[chip]
+    wait_for(rlast, nchip - 1, rr.at[1])
     total = rlast[0]
-    for n in range(1, STRIDE):
+    for n in range(1, nchip):
         total = total + rlast[n]
     for n in range(3 * wx):
         out[n] = total[:, n * wy : (n + 1) * wy]
-    wait_for(rlast, STRIDE - 1, rs.at[1])
+    wait_for(rlast, nchip - 1, rs.at[1])
 
 
 def per_device(background, conductivity, perturbation, coupling, relaxation, receivers, weights):
@@ -604,7 +582,8 @@
     nx_ext = wx + 2 * HALO
     stations = receivers.shape[0]
     depth = nz // naf
-    nblock = naf // STRIDE
+    nchip = naf // CORES
+    group = ngx * ngy
     extended = pltpu.VMEM((2, 2, 3, nx_ext, ROWS, nz), jnp.float32)
     dma = pltpu.SemaphoreType.DMA
     far = pl.BlockSpec(memory_space=pltpu.HBM)
@@ -634,23 +613,19 @@
             pltpu.VMEM((nx_ext * ROWS, stations), jnp.bfloat16),
             pltpu.VMEM((3 * nz, stations), jnp.bfloat16),
             pltpu.VMEM((2, 2, 1, nz), jnp.float32),
-            pltpu.VMEM((2, 2, ngy, 1, nz), jnp.float32),
-            pltpu.VMEM((2, 2, 1, nz), jnp.float32),
-            pltpu.VMEM((2, 2, ngx, 1, nz), jnp.float32),
+            pltpu.VMEM((2, 2, group, 1, nz), jnp.float32),
             pltpu.VMEM((nz, nz), jnp.float32),
-            pltpu.VMEM((nblock, STRIDE, depth, nz), jnp.float32),
-            pltpu.VMEM((nblock, STRIDE, depth, nz), jnp.float32),
-            pltpu.VMEM((STRIDE, depth, nz), jnp.float32),
-            pltpu.VMEM((STRIDE, depth, nz), jnp.float32),
+            pltpu.VMEM((CORES, nchip, depth, nz), jnp.float32),
+            pltpu.VMEM((nchip, depth, nz), jnp.float32),
+            pltpu.VMEM((nchip, depth, nz), jnp.float32),
+            pltpu.VMEM((nchip, depth, nz), jnp.float32),
             dma((8,)),
-            dma((2, 8)),
-            dma((2, 8)),
+            dma((2, 11)),
+            dma((2, 11)),
             dma((8,)),
             dma((8,)),
-            dma((2, 8)),
-            dma((2, 8)),
-            dma((2, 2)),
-            dma((2, 2)),
+            dma((2, 12)),
+            dma((2, 12)),
             dma((2, 2)),
             dma((2, 2)),
             dma((2,)),

time: 55.4 us -> 47.6 us (0.86)
  Pallas kernels: 53.2 us -> 45.4 us
    pallas_call x1, Pallas kernels: 53.2 us -> 45.4 us  [per_device(): pl.pallas_call(functools.partial(kernel, (naf, ngx, ngy, wx, wy, nz)), ou...]
where the time goes in v3:
time: 47.6 us; the launch traced here: 47.4 us
  Pallas kernels  45.4 us (95%)
  local copies, waits for them, and re-layouts  1.35 us (3%)
  between operations  0.66 us (1%)
    pallas_call x1, Pallas kernels, per_device(): pl.pallas_call(functools.partial(kernel, (naf, ngx, ngy, wx, wy, nz)), ou...  45.4 us
    unnamed x1, local copies, waits for them, and re-layouts  1.35 us

profile of v3, /device:TPU:1, one launch (start us, length us, event | category | flops | bytes accessed | tf_op | source)
XLA Modules:
  0.0 47.4 jit_solution(14227828429086674318)
XLA Ops:
  0.7 45.4 %shard_map.73 = f32[12,4,8]{2,1,0:T(4,128)} custom-call(f32[1,2,2,3,4,8,128]{6,5,4,3,2,1,0:T(8,128)} %bg.1, f32[3,4,8,128]{3,2,1,0:T(8,128)} %cond.1, f32[3,4,8,128]{3,2,1,0:T(8,128)} %pert.1, f32[1]{0:T(128)S(6)} %copy.9.coup_hbm, f32[2,3]{1,0:T(2,128)} %relax_hbm.1, s32[8,128]{1,0:T(8,128)} %bitcast.6, f32[8,128]{1,0:T(8,128)} %bitcast.7), custom_call_target="tpu_custom_call" | custom-call | tf_op jit(solution)/shard_map/pallas_call | solution.py:590
  46.1 1.3 %copy.10 = f32[3,4,8,4]{2,3,1,0:T(4,128)} copy(f32[3,4,8,4]{2,3,1,0:T(4,128)} %bitcast.5) | data formatting | bytes 3072

commit v4 on v3

--- a/solution.py
+++ b/solution.py
@@ -162,8 +162,6 @@
     recv_a,
     grad,
     rsend,
-    rfirst,
-    rmid,
     rlast,
     in_sem,
     hs,
@@ -176,14 +174,13 @@
     gar,
     rs,
     rr,
+    known,
 ):
     naf, ngx, ngy, wx, wy, nz = sizes
     af, gx, gy = lax.axis_index("af"), lax.axis_index("gx"), lax.axis_index("gy")
     nx_ext = wx + 2 * HALO
     nspan = naf // (CORES * STRIDE)
     core, high, span = af % CORES, af // CORES % STRIDE, af // (CORES * STRIDE)
-    nchip = nspan * STRIDE
-    chip = span * STRIDE + high
     v1, v2 = Layer(v12, 0), Layer(v12, 1)
 
     def af_of(a_span, a_high, a_core):
@@ -230,17 +227,25 @@
     far_peers = []
     for d_high in (2, 1, 3, 0):
         for d_span in (2, 1, 3, 0):
-            if d_high or d_span:
-                to_span, to_high = span ^ d_span, (high + d_high) % STRIDE
-                far_peers.append(
-                    (to_span * STRIDE + to_high, (af_of(to_span, to_high, core), gx, gy))
-                )
-    for _, device in far_peers:
+            for d_core in (1, 0):
+                if d_high or d_span or d_core:
+                    to = af_of(span ^ d_span, (high + d_high) % STRIDE, core ^ d_core)
+                    far_peers.append((to, (to, gx, gy)))
+    ring_peers = [
+        (af_of(span, (high + d) % STRIDE, core), gx, gy) for d in (1, STRIDE - 1)
+    ] + [(af_of((span + d) % nspan, high, core), gx, gy) for d in (1, nspan - 1)]
+    for device in ring_peers + group_peers + [twin]:
         greet(device)
-    for device in group_peers:
-        greet(device)
-    greet(twin)
-    met = len(far_peers) + len(group_peers) + 1
+    met = len(ring_peers) + len(group_peers) + 1
+
+    def tell(n):
+        for device in ring_peers:
+            pl.semaphore_signal(
+                known.at[n], inc=1, device_id=device, device_id_type=MESH
+            )
+
+    def hear(n):
+        pl.semaphore_wait(known.at[n], len(ring_peers))
 
     loads[0].wait()
     coupled = coup[0]
@@ -314,6 +319,7 @@
     start(halos[0])
     start(halo_d)
     start(halos[1])
+    tell(0)
 
     for load in loads[5:]:
         load.wait()
@@ -466,6 +472,9 @@
                     gram[l, j] = conj(gram[j, l])
         return solve_coefficients(gram, [relax[which, k] for k in range(3)])
 
+    hear(0)
+    tell(1)
+
     for p in range(2):
         wait_recv(halos[p])
         if p == 0:
@@ -475,6 +484,9 @@
         apply(v2, v3, p, X0, X0 + wx, False)
         partial_gram((v0, v1, v2, v3), p, 0)
         start(frames[p])
+
+    hear(1)
+    tell(2)
 
     for p in range(2):
         weights = coefficients(0, p)
@@ -513,6 +525,9 @@
         apply(s2, s3, p, X0, X0 + wx, False)
         partial_gram((s0, s1, s2, s3), p, 1)
 
+    hear(2)
+    tell(3)
+
     grad[3 * wx * wy :] = jnp.zeros((nz - 3 * wx * wy, nz), jnp.float32)
     for p in range(2):
         weights = coefficients(1, p)
@@ -534,19 +549,19 @@
 
     turned = grad[...].T
     depth = nz // naf
-    for a_core in range(CORES):
-        for n in range(nchip):
-            at = (n * CORES + a_core) * depth
-            rsend[a_core, n] = turned[at : at + depth]
-    swap = pltpu.make_async_remote_copy(
-        src_ref=rsend.at[1 - core],
-        dst_ref=rfirst,
-        send_sem=rs.at[0],
-        recv_sem=rr.at[0],
-        device_id=twin,
-        device_id_type=MESH,
-    )
-    swap.start()
+    for n in range(naf):
+        rsend[n] = turned[n * depth : (n + 1) * depth]
+    hear(3)
+    for to, device in far_peers:
+        pltpu.make_async_remote_copy(
+            src_ref=rsend.at[to],
+            dst_ref=rlast.at[af],
+            send_sem=rs.at[0],
+            recv_sem=rr.at[0],
+            device_id=device,
+            device_id_type=MESH,
+        ).start()
+    rlast[af] = rsend[af]
 
     wait_send(halo_d)
     for p in range(2):
@@ -555,25 +570,13 @@
         for which in range(2):
             wait_for(recv_a.at[which, p], group - 1, gas.at[which, p])
 
-    swap.wait()
-    rmid[...] = rsend[core] + rfirst[...]
-    for to, device in far_peers:
-        pltpu.make_async_remote_copy(
-            src_ref=rmid.at[to],
-            dst_ref=rlast.at[chip],
-            send_sem=rs.at[1],
-            recv_sem=rr.at[1],
-            device_id=device,
-            device_id_type=MESH,
-        ).start()
-    rlast[chip] = rmid[chip]
-    wait_for(rlast, nchip - 1, rr.at[1])
+    wait_for(rlast, naf - 1, rr.at[0])
     total = rlast[0]
-    for n in range(1, nchip):
+    for n in range(1, naf):
         total = total + rlast[n]
     for n in range(3 * wx):
         out[n] = total[:, n * wy : (n + 1) * wy]
-    wait_for(rlast, nchip - 1, rs.at[1])
+    wait_for(rlast, naf - 1, rs.at[0])
 
 
 def per_device(background, conductivity, perturbation, coupling, relaxation, receivers, weights):
@@ -582,7 +585,6 @@
     nx_ext = wx + 2 * HALO
     stations = receivers.shape[0]
     depth = nz // naf
-    nchip = naf // CORES
     group = ngx * ngy
     extended = pltpu.VMEM((2, 2, 3, nx_ext, ROWS, nz), jnp.float32)
     dma = pltpu.SemaphoreType.DMA
@@ -615,10 +617,8 @@
             pltpu.VMEM((2, 2, 1, nz), jnp.float32),
             pltpu.VMEM((2, 2, group, 1, nz), jnp.float32),
             pltpu.VMEM((nz, nz), jnp.float32),
-            pltpu.VMEM((CORES, nchip, depth, nz), jnp.float32),
-            pltpu.VMEM((nchip, depth, nz), jnp.float32),
-            pltpu.VMEM((nchip, depth, nz), jnp.float32),
-            pltpu.VMEM((nchip, depth, nz), jnp.float32),
+            pltpu.VMEM((naf, depth, nz), jnp.float32),
+            pltpu.VMEM((naf, depth, nz), jnp.float32),
             dma((8,)),
             dma((2, 11)),
             dma((2, 11)),
@@ -628,8 +628,9 @@
             dma((2, 12)),
             dma((2, 2)),
             dma((2, 2)),
-            dma((2,)),
-            dma((2,)),
+            dma((1,)),
+            dma((1,)),
+            pltpu.SemaphoreType.REGULAR((4,)),
         ],
         compiler_params=pltpu.CompilerParams(
             collective_id=0, has_side_effects=True, vmem_limit_bytes=62 * 1024 * 1024

time: 47.6 us -> 46.8 us (0.983)
  Pallas kernels: 45.4 us -> 44.6 us
    pallas_call x1, Pallas kernels: 45.4 us -> 44.6 us  [per_device(): pl.pallas_call(functools.partial(kernel, (naf, ngx, ngy, wx, wy, nz)), ou...]
where the time goes in v4:
time: 46.8 us; the launch traced here: 46.6 us
  Pallas kernels  44.6 us (95%)
  local copies, waits for them, and re-layouts  1.35 us (3%)
  between operations  0.66 us (1%)
    pallas_call x1, Pallas kernels, per_device(): pl.pallas_call(functools.partial(kernel, (naf, ngx, ngy, wx, wy, nz)), ou...  44.6 us
    unnamed x1, local copies, waits for them, and re-layouts  1.35 us

profile of v4, /device:TPU:1, one launch (start us, length us, event | category | flops | bytes accessed | tf_op | source)
XLA Modules:
  0.0 46.6 jit_solution(13760488897923047871)
XLA Ops:
  0.7 44.6 %shard_map.73 = f32[12,4,8]{2,1,0:T(4,128)} custom-call(f32[1,2,2,3,4,8,128]{6,5,4,3,2,1,0:T(8,128)} %bg.1, f32[3,4,8,128]{3,2,1,0:T(8,128)} %cond.1, f32[3,4,8,128]{3,2,1,0:T(8,128)} %pert.1, f32[1]{0:T(128)S(6)} %copy.9.coup_hbm, f32[2,3]{1,0:T(2,128)} %relax_hbm.1, s32[8,128]{1,0:T(8,128)} %bitcast.6, f32[8,128]{1,0:T(8,128)} %bitcast.7), custom_call_target="tpu_custom_call" | custom-call | tf_op jit(solution)/shard_map/pallas_call | solution.py:592
  45.3 1.3 %copy.10 = f32[3,4,8,4]{2,3,1,0:T(4,128)} copy(f32[3,4,8,4]{2,3,1,0:T(4,128)} %bitcast.5) | data formatting | bytes 3072

commit v5 on v4

--- a/solution.py
+++ b/solution.py
@@ -201,9 +201,6 @@
             )
         )
     ]
-    for load in loads:
-        load.start()
-
     zeros = jnp.zeros((ROWS, nz), jnp.float32)
     for i in range(nx_ext):
         for p in range(2):
@@ -234,7 +231,11 @@
     ring_peers = [
         (af_of(span, (high + d) % STRIDE, core), gx, gy) for d in (1, STRIDE - 1)
     ] + [(af_of((span + d) % nspan, high, core), gx, gy) for d in (1, nspan - 1)]
-    for device in ring_peers + group_peers + [twin]:
+    for device in ring_peers[:2] + group_peers:
+        greet(device)
+    for load in loads:
+        load.start()
+    for device in ring_peers[2:] + [twin]:
         greet(device)
     met = len(ring_peers) + len(group_peers) + 1
 

time: 46.8 us -> 46.8 us (level)
  no operation moved by 1% of the time
where the time goes in v5:
time: 46.8 us; the launch traced here: 46.6 us
  Pallas kernels  44.6 us (95%)
  local copies, waits for them, and re-layouts  1.35 us (3%)
  between operations  0.66 us (1%)
    pallas_call x1, Pallas kernels, per_device(): pl.pallas_call(functools.partial(kernel, (naf, ngx, ngy, wx, wy, nz)), ou...  44.6 us
    unnamed x1, local copies, waits for them, and re-layouts  1.35 us

profile of v5, /device:TPU:1, one launch (start us, length us, event | category | flops | bytes accessed | tf_op | source)
XLA Modules:
  0.0 46.6 jit_solution(15264470176209905880)
XLA Ops:
  0.7 44.6 %shard_map.73 = f32[12,4,8]{2,1,0:T(4,128)} custom-call(f32[1,2,2,3,4,8,128]{6,5,4,3,2,1,0:T(8,128)} %bg.1, f32[3,4,8,128]{3,2,1,0:T(8,128)} %cond.1, f32[3,4,8,128]{3,2,1,0:T(8,128)} %pert.1, f32[1]{0:T(128)S(6)} %copy.9.coup_hbm, f32[2,3]{1,0:T(2,128)} %relax_hbm.1, s32[8,128]{1,0:T(8,128)} %bitcast.6, f32[8,128]{1,0:T(8,128)} %bitcast.7), custom_call_target="tpu_custom_call" | custom-call | tf_op jit(solution)/shard_map/pallas_call | solution.py:593
  45.2 1.3 %copy.10 = f32[3,4,8,4]{2,3,1,0:T(4,128)} copy(f32[3,4,8,4]{2,3,1,0:T(4,128)} %bitcast.5) | data formatting | bytes 3072

commit v6 on v5

--- a/solution.py
+++ b/solution.py
@@ -529,7 +529,6 @@
     hear(2)
     tell(3)
 
-    grad[3 * wx * wy :] = jnp.zeros((nz - 3 * wx * wy, nz), jnp.float32)
     for p in range(2):
         weights = coefficients(1, p)
         wide = [tuple(jnp.broadcast_to(v, (wy, nz)) for v in w) for w in weights]
@@ -548,10 +547,17 @@
                 at = slice((k * wx + i) * wy, (k * wx + i + 1) * wy)
                 grad[at] = product if p == 0 else grad[at] + product
 
+    depth = nz // naf
+    third = wx * wy
+    layer = lax.broadcasted_iota(jnp.int32, (third, nz), 1) % depth
+    fourth = jnp.zeros((third, nz), jnp.float32)
+    for k in range(3):
+        moved = pltpu.roll(grad[k * third : (k + 1) * third], nz - 3 + k, 1)
+        fourth = jnp.where(layer == k, moved, fourth)
+    grad[3 * third :] = fourth
     turned = grad[...].T
-    depth = nz // naf
     for n in range(naf):
-        rsend[n] = turned[n * depth : (n + 1) * depth]
+        rsend[n] = turned[n * depth : n * depth + 3]
     hear(3)
     for to, device in far_peers:
         pltpu.make_async_remote_copy(
@@ -576,7 +582,9 @@
     for n in range(1, naf):
         total = total + rlast[n]
     for n in range(3 * wx):
-        out[n] = total[:, n * wy : (n + 1) * wy]
+        k, at = n // wx, 3 * third + n % wx * wy
+        out[n, 0:3] = total[:, n * wy : (n + 1) * wy]
+        out[n, 3:4] = total[k : k + 1, at : at + wy]
     wait_for(rlast, naf - 1, rs.at[0])
 
 
@@ -618,8 +626,8 @@
             pltpu.VMEM((2, 2, 1, nz), jnp.float32),
             pltpu.VMEM((2, 2, group, 1, nz), jnp.float32),
             pltpu.VMEM((nz, nz), jnp.float32),
-            pltpu.VMEM((naf, depth, nz), jnp.float32),
-            pltpu.VMEM((naf, depth, nz), jnp.float32),
+            pltpu.VMEM((naf, 3, nz), jnp.float32),
+            pltpu.VMEM((naf, 3, nz), jnp.float32),
             dma((8,)),
             dma((2, 11)),
             dma((2, 11)),

time: 46.8 us -> 46.8 us (level)
  no operation moved by 1% of the time
where the time goes in v6:
time: 46.8 us; the launch traced here: 46.6 us
  Pallas kernels  44.6 us (95%)
  local copies, waits for them, and re-layouts  1.35 us (3%)
  between operations  0.66 us (1%)
    pallas_call x1, Pallas kernels, per_device(): pl.pallas_call(functools.partial(kernel, (naf, ngx, ngy, wx, wy, nz)), ou...  44.6 us
    unnamed x1, local copies, waits for them, and re-layouts  1.35 us

profile of v6, /device:TPU:1, one launch (start us, length us, event | category | flops | bytes accessed | tf_op | source)
XLA Modules:
  0.0 46.6 jit_solution(9573210795505936134)
XLA Ops:
  0.7 44.6 %shard_map.73 = f32[12,4,8]{2,1,0:T(4,128)} custom-call(f32[1,2,2,3,4,8,128]{6,5,4,3,2,1,0:T(8,128)} %bg.1, f32[3,4,8,128]{3,2,1,0:T(8,128)} %cond.1, f32[3,4,8,128]{3,2,1,0:T(8,128)} %pert.1, f32[1]{0:T(128)S(6)} %copy.9.coup_hbm, f32[2,3]{1,0:T(2,128)} %relax_hbm.1, s32[8,128]{1,0:T(8,128)} %bitcast.6, f32[8,128]{1,0:T(8,128)} %bitcast.7), custom_call_target="tpu_custom_call" | custom-call | tf_op jit(solution)/shard_map/pallas_call | solution.py:601
  45.3 1.3 %copy.10 = f32[3,4,8,4]{2,3,1,0:T(4,128)} copy(f32[3,4,8,4]{2,3,1,0:T(4,128)} %bitcast.5) | data formatting | bytes 3072
